TPU v7x, 256 devices: a whole 4x4x8 slice. The times are simulated.
256 devices in a mesh: batch: 16 (over z_hi, y, core), dap: 16 (over z_lo, x).
Axes of the slice: x: 4, y: 4, z: 8 (z_hi: 2, z_lo: 4; z = z_hi * 4 + z_lo), core: 2. Of those that a mesh axis runs over, the one named last changes fastest.
Arguments:
- alignment: bfloat16 [32, 128, 256, 256], P('batch', 'dap'), may hold values from -6 to 6
- cotangent: bfloat16 [32, 128, 256, 256], P('batch', 'dap'), may hold values from -6 to 6
- query_weight: bfloat16 [256, 256], replicated, may hold values from -3 to 3
- key_weight: bfloat16 [256, 256], replicated, may hold values from -3 to 3
- value_weight: bfloat16 [256, 256], replicated, may hold values from -0.375 to 0.375
- gate_weight: bfloat16 [256, 256], replicated, may hold values from -0.375 to 0.375
- gate_bias: float32 [256], replicated, may hold values from -4 to 4
- out_weight: bfloat16 [256, 256], replicated, may hold values from -0.375 to 0.375
- out_bias: float32 [256], replicated, may hold values from -3 to 3
- ln_gain: float32 [256], replicated, may hold values from 0.1 to 1.9
- ln_bias: float32 [256], replicated, may hold values from -3 to 3
Outputs:
- updated: bfloat16 [32, 128, 256, 256], P('batch', 'dap')
- grad_alignment: bfloat16 [32, 128, 256, 256], P('batch', 'dap')
- grad_projections: float32 [4, 256, 256], replicated
- grad_output: float32 [256, 256], replicated
- grad_vectors: float32 [4, 256], replicated
All inputs are finite; a program needn't handle non-finite values.
Results may differ from a plain program's by a relative error of at most 0.012.
The roundings to bfloat16 on the way count: a program that leaves them out, or rounds other values in their place, can miss the bound.
Values may be sent and summed in bfloat16 or wider, within the bound.
No kernel may reach another device: no remote copies, remote signals or barrier semaphores. Data moves between devices by JAX's collectives and lax.ppermute only.
A program may use at most 128 MiB of HBM per device.

v0:
```python
import functools
import math

import jax
import jax.numpy as jnp
from jax import lax
from jax.experimental import pallas as pl
from jax.experimental.pallas import tpu as pltpu
from jax.sharding import Mesh
from jax.sharding import PartitionSpec as P

C = 256
HEADS = 8
HDIM = 32
ROWS = 128
RES = 256
HD = 256
STRUCTS = 32
EPSILON = 1e-05
INV_SCALE = 1.0 / math.sqrt(HDIM)
FACTOR = 1.0 / math.sqrt(STRUCTS * ROWS * RES)
F32 = jnp.float32
BF16 = jnp.bfloat16

MEMBERS = 16
OWN_ROWS = ROWS // MEMBERS
UNITS = 4
PAIRS = 2
STEPS = 2
DAP = ("z_lo", "x")
BATCH = ("z_hi", "y", "core")
RING = ("z_hi", "z_lo")
TILES = 176
GROUP = 16
COUNT = GROUP * 2 * PAIRS
VMEM = 60 * 2**20


def dot(left, right, left_dim=1, right_dim=0):
    return lax.dot_general(
        left, right, (((left_dim,), (right_dim,)), ((), ())), preferred_element_type=F32
    )


def unit_specs(first):
    rows = pl.BlockSpec(
        (1, OWN_ROWS, COUNT, C),
        lambda n, g: ((first + n) // UNITS, 0, (first + n) % UNITS * (MEMBERS // GROUP) + g, 0),
    )
    packed = pl.BlockSpec((GROUP, 2, PAIRS, 16, C), lambda n, g: (g, 0, n, 0, 0))
    return rows, packed


def pack_kernel(x_ref, cot_ref, out_ref, wide):
    for which, ref in enumerate((x_ref, cot_ref)):
        for side in range(2):
            lanes = slice(side * 128, side * 128 + 128)
            for row in range(OWN_ROWS):
                wide[which, side, pl.ds(row, COUNT, stride=OWN_ROWS), :] = ref[0, row, :, lanes].astype(F32)
            out_ref[:, which, :, :, lanes] = wide[which, side].reshape(GROUP, PAIRS, 16, 128).astype(BF16)


def pack(alignment, cotangent, first, units):
    rows, packed = unit_specs(first)
    return pl.pallas_call(
        pack_kernel,
        grid=(units, MEMBERS // GROUP),
        in_specs=[rows, rows],
        out_specs=packed,
        out_shape=pltpu.HBM((MEMBERS, 2, units * PAIRS, 16, C), BF16),
        scratch_shapes=[pltpu.VMEM((2, 2, COUNT * OWN_ROWS, 128), F32)],
        compiler_params=pltpu.CompilerParams(vmem_limit_bytes=VMEM),
        cost_estimate=pl.CostEstimate(flops=0, bytes_accessed=units * 2**21, transcendentals=0),
    )(alignment, cotangent)


def unpack_kernel(*refs):
    in_ref, upd_ref, grad_ref, wide = refs[0], *refs[-3:]
    for which, ref in enumerate((upd_ref, grad_ref)):
        for side in range(2):
            lanes = slice(side * 128, side * 128 + 128)
            wide[which, side] = in_ref[:, which, :, :, lanes].astype(F32).reshape(COUNT * OWN_ROWS, 128)
            for row in range(OWN_ROWS):
                ref[0, row, :, lanes] = wide[
                    which, side, pl.ds(row, COUNT, stride=OWN_ROWS), :
                ].astype(BF16)


def unpack(packed, first, structs, earlier):
    rows, blocks = unit_specs(first)
    shape = pltpu.HBM((structs, OWN_ROWS, RES, C), BF16)
    units = packed.shape[2] // PAIRS
    return pl.pallas_call(
        unpack_kernel,
        grid=(units, MEMBERS // GROUP),
        in_specs=[blocks] + [pl.BlockSpec(memory_space=pl.ANY)] * len(earlier),
        out_specs=[rows, rows],
        out_shape=[shape, shape],
        input_output_aliases={1 + k: k for k in range(len(earlier))},
        scratch_shapes=[pltpu.VMEM((2, 2, COUNT * OWN_ROWS, 128), F32)],
        compiler_params=pltpu.CompilerParams(vmem_limit_bytes=24 * 2**20),
        cost_estimate=pl.CostEstimate(flops=0, bytes_accessed=units * 2**21, transcendentals=0),
    )(packed, *earlier)


def token_rows(block):
    wide = block.astype(F32)
    return jnp.concatenate(
        [
            wide[:, pair, side : side + 8].reshape(ROWS, C)
            for pair in range(block.shape[1])
            for side in (0, 8)
        ],
        axis=0,
    )


def row_blocks(tokens, pair):
    first = tokens[2 * pair * ROWS : (2 * pair + 1) * ROWS].reshape(MEMBERS, 8, C)
    other = tokens[(2 * pair + 1) * ROWS : (2 * pair + 2) * ROWS].reshape(MEMBERS, 8, C)
    return jnp.concatenate([first, other], axis=1)


def fold_rows(tokens):
    return jnp.sum(tokens.reshape(tokens.shape[0] // 8, 8, C), axis=0)


def tiles_of(matrix):
    count = matrix.shape[0] // 8
    return matrix[:, :128].reshape(count, 8, 128), matrix[:, 128:].reshape(count, 8, 128)


def pair_kernel(steps, has_earlier, last, *refs):
    core_ref, x_ref, cot_ref, w_ref, wt_ref, wo_ref, gb_ref, rows_ref = refs[:8]
    qc, kc, vc, dac, attc, dprojc, gin, gout, vec, dlog = refs[-10:]
    if last:
        out_ref, own_ref, other_ref, sums_ref, refs = *refs[-14:-10], refs[:-10]
    else:
        out_ref, sums_ref = refs[-12:-10]

    @pl.when(pl.program_id(0) == 0)
    def _():
        gin[...] = jnp.zeros_like(gin)
        gout[...] = jnp.zeros_like(gout)
        vec[...] = jnp.zeros_like(vec)
        dlog[...] = jnp.zeros_like(dlog)

    pairs = x_ref.shape[2]
    out_bias, gain, bias = rows_ref[0:1], rows_ref[1:2], rows_ref[2:3]
    x = token_rows(x_ref[:, 0])
    cot = token_rows(cot_ref[:, 0])
    cot_half = cot.astype(BF16)
    centered = x - jnp.mean(x, axis=-1, keepdims=True)
    inv_std = lax.rsqrt(jnp.mean(centered * centered, axis=-1, keepdims=True) + EPSILON)
    standard = centered * inv_std
    normed = (standard * gain + bias).astype(BF16)

    kv = dot(normed, w_ref[:, HD : 3 * HD]).astype(BF16)
    proj = dot(wt_ref[...], normed, 1, 1)
    qc[...] = (proj[:HD] * INV_SCALE).astype(BF16)
    kc[...] = proj[HD : 2 * HD].astype(BF16)
    vc[...] = proj[2 * HD : 3 * HD].astype(BF16)
    gate = jax.nn.sigmoid(proj[3 * HD :] + jnp.concatenate([gb_ref[...]] * (2 * pairs), axis=1))
    d_gated = dot(wo_ref[...], cot_half, 1, 1)
    dac[...] = (d_gated * gate).astype(BF16)

    head_of_lane = lax.broadcasted_iota(jnp.int32, (1, 128), 1) // HDIM
    for r in range(2 * pairs):
        toks = slice(r * ROWS, (r + 1) * ROWS)
        for half in range(2):
            lanes = slice(half * 128, half * 128 + 128)
            k_half = kv[toks, half * 128 : half * 128 + 128]
            v_half = kv[toks, HD + half * 128 : HD + half * 128 + 128]
            zero = jnp.zeros_like(k_half)
            k_stack = jnp.concatenate(
                [jnp.where(head_of_lane == h, k_half, zero) for h in range(4)], axis=0
            )
            v_stack = jnp.concatenate(
                [jnp.where(head_of_lane == h, v_half, zero) for h in range(4)], axis=0
            )
            scores = dot(k_stack, qc[lanes, toks])
            d_softs = dot(v_stack, dac[lanes, toks])
            for hp in range(2):
                probs, d_ss = [], []
                for h in (2 * hp, 2 * hp + 1):
                    s = scores[h * 128 : h * 128 + 128]
                    d_soft = d_softs[h * 128 : h * 128 + 128]
                    shifted = jnp.exp(s - jnp.max(s, axis=0, keepdims=True))
                    soft = shifted * (1.0 / jnp.sum(shifted, axis=0, keepdims=True))
                    weighted = soft * d_soft
                    d_s = (weighted - soft * jnp.sum(weighted, axis=0, keepdims=True)).astype(BF16)
                    probs.append(soft.astype(BF16))
                    d_ss.append(d_s)
                probs = jnp.concatenate(probs, axis=0)
                d_ss = jnp.concatenate(d_ss, axis=0)
                f = half * 128 + hp * 2 * HDIM
                chans = slice(f, f + 2 * HDIM)
                hole = jnp.zeros((HDIM, ROWS), BF16)

                def diagonal(rows):
                    return jnp.concatenate(
                        [
                            jnp.concatenate([rows[:HDIM], hole], axis=1),
                            jnp.concatenate([hole, rows[HDIM:]], axis=1),
                        ],
                        axis=0,
                    )

                def blocks(wide):
                    return jnp.concatenate([wide[:HDIM, :ROWS], wide[HDIM:, ROWS:]], axis=0)

                attc[chans, toks] = dot(diagonal(vc[chans, toks]), probs)
                dprojc[chans, toks] = (dot(diagonal(kc[chans, toks]), d_ss) * INV_SCALE).astype(BF16)
                dprojc[HD + f : HD + f + 2 * HDIM, toks] = blocks(dot(qc[chans, toks], d_ss, 1, 1)).astype(BF16)
                dprojc[2 * HD + f : 2 * HD + f + 2 * HDIM, toks] = blocks(
                    dot(dac[chans, toks], probs, 1, 1)
                ).astype(BF16)


    gated = gate * attc[...]
    d_logit = (d_gated * gated * (1.0 - gate)).astype(BF16)
    dprojc[3 * HD :, :] = d_logit
    gated_half = gated.astype(BF16)
    wide_logit = d_logit.astype(F32)
    dlog[...] += functools.reduce(
        jnp.add, [wide_logit[:, r * ROWS : (r + 1) * ROWS] for r in range(2 * pairs)]
    )
    gin[...] += dot(dprojc[...], normed)
    gout[...] += dot(gated_half, cot_half)
    update = dot(gated_half.T, wo_ref[...]) + out_bias
    updated = x + update
    d_normed = dot(w_ref[...], dprojc[...]).T
    d_hat = d_normed * gain
    d_std = d_normed * standard
    branch = inv_std * (
        d_hat
        - jnp.mean(d_hat, axis=-1, keepdims=True)
        - standard * jnp.mean(d_hat * standard, axis=-1, keepdims=True)
    )
    grad = cot + branch
    for pair in range(pairs):
        out_ref[:, 0, pair] = row_blocks(updated, pair).astype(BF16)
        out_ref[:, 1, pair] = row_blocks(grad, pair).astype(BF16)
    vec[0] += fold_rows(cot)
    vec[1] += fold_rows(d_std)
    vec[2] += fold_rows(d_normed)

    @pl.when(pl.program_id(0) == steps - 1)
    def _():
        def put(half, first, tiles):
            count = tiles.shape[0]
            if has_earlier:
                tiles = tiles + refs[8][half, first : first + count]
            sums_ref[half, first : first + count] = tiles

        for block in range(5):
            matrix = gin[block * HD : (block + 1) * HD].T if block < 4 else gout[...]
            for half, tiles in enumerate(tiles_of(matrix)):
                put(half, block * 32, tiles)
        rows = [jnp.sum(dlog[...].T, axis=0, keepdims=True)] + [
            jnp.sum(vec[k], axis=0, keepdims=True) for k in range(3)
        ]
        vectors = [row[:, side : side + 128] for row in rows for side in (0, 128)]
        put(0, 160, jnp.concatenate(vectors, axis=0)[None])
        sums_ref[0, 161:] = jnp.zeros((TILES - 161, 8, 128), F32)
        sums_ref[1, 160:] = jnp.zeros((TILES - 160, 8, 128), F32)
        if last:
            core = core_ref[0]
            own_ref[...] = sums_ref[core]
            other_ref[...] = sums_ref[1 - core]


def columns(packed, core, params, sums=None, last=False):
    pairs = packed.shape[2] // STEPS

    def part(which):
        return pl.BlockSpec((MEMBERS, 1, pairs, 16, C), lambda p: (0, which, p, 0, 0))

    def whole(shape):
        return pl.BlockSpec(shape, lambda p: (0,) * len(shape))

    half = (TILES, 8, 128)
    operands = [core, packed, packed, *params]
    in_specs = [pl.BlockSpec(memory_space=pltpu.SMEM), part(0), part(1)] + [whole(a.shape) for a in params]
    if sums is not None:
        operands.append(sums)
        in_specs.append(whole(sums.shape))
    out_specs = [pl.BlockSpec((MEMBERS, 2, pairs, 16, C), lambda p: (0, 0, p, 0, 0))]
    out_shape = [pltpu.HBM(packed.shape, BF16)]
    wide = (HD, 2 * pairs * ROWS)
    scratch = [pltpu.VMEM(wide, BF16)] * 4 + [
        pltpu.VMEM(wide, F32),
        pltpu.VMEM((4 * HD, 2 * pairs * ROWS), BF16),
        pltpu.VMEM((4 * HD, C), F32),
        pltpu.VMEM((HD, C), F32),
        pltpu.VMEM((3, 8, C), F32),
        pltpu.VMEM((HD, 128), F32),
    ]
    if last:
        out_specs += [whole(half)] * 2
        out_shape += [pltpu.HBM(half, F32)] * 2
        scratch.insert(0, pltpu.VMEM((2, *half), F32))
    else:
        out_specs.append(whole((2, *half)))
        out_shape.append(pltpu.HBM((2, *half), F32))
    return pl.pallas_call(
        functools.partial(pair_kernel, STEPS, sums is not None, last),
        grid=(STEPS,),
        in_specs=in_specs,
        out_specs=out_specs,
        out_shape=out_shape,
        scratch_shapes=scratch,
        compiler_params=pltpu.CompilerParams(
            dimension_semantics=("arbitrary",), vmem_limit_bytes=VMEM
        ),
        cost_estimate=pl.CostEstimate(
            flops=packed.shape[2] * 4_000_000_000, bytes_accessed=2**23, transcendentals=packed.shape[2] * 300_000
        ),
    )(*operands)


def shift(value, axes, size, step):
    return lax.ppermute(value, axes, [(k, (k + step) % size) for k in range(size)])


def scatter_sum(terms, axes, size):
    own = lax.axis_index(axes)
    count = terms[0].shape[0] // size

    def block_for(step):
        place = lax.rem(own + step, size) * count
        return functools.reduce(
            jnp.add, [lax.dynamic_slice_in_dim(term, place, count, 0) for term in terms]
        )

    arrived = [shift(block_for(step), axes, size, step) for step in range(1, size)]
    return functools.reduce(jnp.add, arrived, block_for(0))


def gather(value, axes, size):
    own = lax.axis_index(axes)
    count = value.shape[0]
    arrived = [shift(value, axes, size, step) for step in range(1, size)]
    total = jnp.zeros((size * count, *value.shape[1:]), value.dtype)
    for step, piece in enumerate([value, *arrived]):
        place = lax.rem(own + size - step, size) * count
        total = lax.dynamic_update_slice_in_dim(total, piece, place, 0)
    return total


def swap(value, axis):
    return lax.ppermute(value, axis, [(0, 1), (1, 0)])


def meet_sum(value, axes, size):
    own = lax.axis_index(axes)
    arrived = [shift(value, axes, size, step) for step in range(1, size)]
    met = jnp.concatenate([value, *arrived], axis=0).reshape(size, *value.shape)
    pieces = [
        lax.dynamic_index_in_dim(met, lax.rem(own + size - k, size), 0, keepdims=False)
        for k in range(size)
    ]
    return functools.reduce(jnp.add, pieces)


def finish_kernel(core_ref, own_ref, other_ref, mats_ref, out_ref, vec_ref):
    def write(halves):
        for half, ref in enumerate(halves):
            lanes = slice(half * 128, half * 128 + 128)
            for block in range(4):
                mats_ref[block, :, lanes] = ref[block * 32 : block * 32 + 32].reshape(C, 128)
            out_ref[:, lanes] = ref[128:160].reshape(C, 128)
        for k in range(8):
            vec_ref[k // 2 : k // 2 + 1, k % 2 * 128 : k % 2 * 128 + 128] = halves[0][160, k : k + 1]

    pl.when(core_ref[0] == 0)(lambda: write((own_ref, other_ref)))
    pl.when(core_ref[0] == 1)(lambda: write((other_ref, own_ref)))


def finish(core, own, other):
    vmem = pl.BlockSpec(memory_space=pltpu.VMEM)
    return pl.pallas_call(
        finish_kernel,
        in_specs=[pl.BlockSpec(memory_space=pltpu.SMEM), vmem, vmem],
        out_specs=[vmem] * 3,
        out_shape=[
            jax.ShapeDtypeStruct((4, C, HD), F32),
            jax.ShapeDtypeStruct((HD, C), F32),
            jax.ShapeDtypeStruct((4, C), F32),
        ],
        compiler_params=pltpu.CompilerParams(vmem_limit_bytes=16 * 2**20),
        cost_estimate=pl.CostEstimate(flops=0, bytes_accessed=2**22, transcendentals=0),
    )(core, own, other)


def rows_sum(own, other):
    tiles = scatter_sum([own, swap(other, "core")], "y", 4)
    return scatter_sum([tiles], "x", 4)


def shards(alignment, cotangent, wq, wk, wv, wg, gate_bias, wo, out_bias, gain, bias):
    structs = alignment.shape[0]
    w = jnp.concatenate([wq, wk, wv, wg], axis=1)
    rows = jnp.concatenate([jnp.stack([out_bias, gain, bias]), jnp.zeros((5, C), F32)], axis=0)
    params = (w, w.T, wo, jnp.broadcast_to(gate_bias[:, None], (HD, 128)), rows)
    core = lax.axis_index("core").reshape(1)
    after = lax.optimization_barrier

    def exchange(value):
        return lax.all_to_all(value, DAP, 0, 0, tiled=True)

    first = exchange(pack(alignment, cotangent, 0, 5))
    second = exchange(pack(alignment, cotangent, 5, 3))
    early, sums = columns(first, core, params)
    early = exchange(early)
    late, own, other = columns(second, core, params, sums, last=True)
    tiles = rows_sum(own, other)
    tiles = (tiles + swap(tiles, "z_hi")) * FACTOR
    tiles, late = after((meet_sum(tiles, "z_lo", 4), late))
    late = exchange(late)
    done = unpack(early, 0, structs, ())
    for axis in ("x", "y"):
        tiles = gather(tiles, axis, 4)
    mats, out, vectors = finish(core, tiles, swap(tiles, "core"))
    return (*unpack(late, 5, structs, tuple(done)), mats, out, vectors)


def solution(mesh):
    parts = Mesh(mesh.devices.reshape(2, 4, 2, 4, 4), BATCH + DAP)
    split = P(BATCH, DAP, None, None)
    return jax.shard_map(
        shards,
        mesh=parts,
        in_specs=(split, split) + (P(),) * 9,
        out_specs=(split, split, P(), P(), P()),
        check_vma=False,
    )
```

profile of v0, /device:TPU:32, one launch (start us, length us, event | category | flops | bytes accessed | tf_op | source)
XLA Modules:
  0.0 230.9 jit_solution(3999527267305988983)
XLA Ops:
  0.6 5.3 %shard_map.147 = bf16[16,2,10,16,256]{4,3,2,1,0:T(8,128)(2,1)} custom-call(bf16[2,8,256,256]{3,2,1,0:T(8,128)(2,1)} %x_ref.3, bf16[2,8,256,256]{3,2,1,0:T(8,128)(2,1)} %cot_ref.3), custom_call_target="tpu_custom_call" | custom-call | bytes 10485760 | tf_op jit(solution)/shard_map/pallas_call | solution.py:65
  5.9 8.5 %all-to-all-start.1 = ((bf16[16,2,10,16,256]{4,3,2,1,0:T(8,128)(2,1)}), bf16[16,2,10,16,256]{4,3,2,1,0:T(8,128)(2,1)S(1)}, u32[]{:S(2)}, u32[]{:S(2)}) async-start(bf16[16,2,10,16,256]{4,3,2,1,0:T(8,128)(2,1)} %shard_map.147), calls=%async_computation.1 | async-start | bytes 5242880 | tf_op jit(solution)/shard_map/all_to_all | solution.py:410
  14.5 3.8 %shard_map.146 = bf16[16,2,6,16,256]{4,3,2,1,0:T(8,128)(2,1)} custom-call(bf16[2,8,256,256]{3,2,1,0:T(8,128)(2,1)} %x_ref.3, bf16[2,8,256,256]{3,2,1,0:T(8,128)(2,1)} %cot_ref.3), custom_call_target="tpu_custom_call" | custom-call | bytes 6291456 | tf_op jit(solution)/shard_map/pallas_call | solution.py:65
  19.4 1.8 fusion
  23.0 49.4 %all-to-all-done.1.refs_1_.refs_2_ = bf16[16,2,10,16,256]{4,3,2,1,0:T(8,128)(2,1)S(1)} async-done(((bf16[16,2,10,16,256]{4,3,2,1,0:T(8,128)(2,1)}), bf16[16,2,10,16,256]{4,3,2,1,0:T(8,128)(2,1)S(1)}, u32[]{:S(2)}, u32[]{:S(2)}) %all-to-all-start.1) | async-done | bytes 2621472 | tf_op jit(solution)/shard_map/all_to_all | solution.py:410
  72.4 6.7 %all-to-all-start = ((bf16[16,2,6,16,256]{4,3,2,1,0:T(8,128)(2,1)}), bf16[16,2,6,16,256]{4,3,2,1,0:T(8,128)(2,1)}, u32[]{:S(2)}, u32[]{:S(2)}) async-start(bf16[16,2,6,16,256]{4,3,2,1,0:T(8,128)(2,1)} %shard_map.146), calls=%async_computation | async-start | bytes 3145728 | tf_op jit(solution)/shard_map/all_to_all | solution.py:410
  79.9 25.9 %shard_map.148 = (bf16[16,2,10,16,256]{4,3,2,1,0:T(8,128)(2,1)}, f32[2,176,8,128]{3,2,1,0:T(8,128)}) custom-call(s32[1]{0:T(128)} %bitcast.refs_0_.core_ref, bf16[16,2,10,16,256]{4,3,2,1,0:T(8,128)(2,1)} %copy-done, bf16[16,2,10,16,256]{4,3,2,1,0:T(8,128)(2,1)} %copy-done, bf16[256,1024]{1,0:T(8,128)(2,1)} %copy.23.refs_3_, ...), custom_call_target="tpu_custom_call" | custom-call | flops 40000000000 | bytes 8388608 | tf_op jit(solution)/shard_map/pallas_call | solution.py:306
  105.8 9.3 %all-to-all-done.refs_1_.refs_2_ = bf16[16,2,6,16,256]{4,3,2,1,0:T(8,128)(2,1)} async-done(((bf16[16,2,6,16,256]{4,3,2,1,0:T(8,128)(2,1)}), bf16[16,2,6,16,256]{4,3,2,1,0:T(8,128)(2,1)}, u32[]{:S(2)}, u32[]{:S(2)}) %all-to-all-start) | async-done | bytes 1572896 | tf_op jit(solution)/shard_map/all_to_all | solution.py:410
  115.1 5.5 %all-to-all-start.3 = ((bf16[16,2,10,16,256]{4,3,2,1,0:T(8,128)(2,1)}), bf16[16,2,10,16,256]{4,3,2,1,0:T(8,128)(2,1)S(1)}, u32[]{:S(2)}, u32[]{:S(2)}) async-start(bf16[16,2,10,16,256]{4,3,2,1,0:T(8,128)(2,1)} %get-tuple-element.24), calls=%async_computation.3 | async-start | bytes 5242880 | tf_op jit(solution)/shard_map/all_to_all | solution.py:410
  120.6 17.8 %shard_map.149 = (bf16[16,2,6,16,256]{4,3,2,1,0:T(8,128)(2,1)}, f32[176,8,128]{2,1,0:T(8,128)}, f32[176,8,128]{2,1,0:T(8,128)}) custom-call(s32[1]{0:T(128)} %bitcast.refs_0_.core_ref, bf16[16,2,6,16,256]{4,3,2,1,0:T(8,128)(2,1)} %all-to-all-done.refs_1_.refs_2_, bf16[16,2,6,16,256]{4,3,2,1,0:T(8,128)(2,1)} %all-to-all-done.refs_1_.refs_2_, ...), custom_call_target="tpu_custom_call" | custom-call | flops 24000000000 | bytes 8388608 | tf_op jit(solution)/shard_map/pallas_call | solution.py:306
  138.5 2.4 %collective-permute-done = f32[176,8,128]{2,1,0:T(8,128)S(1)} collective-permute-done((f32[176,8,128]{2,1,0:T(8,128)}, f32[176,8,128]{2,1,0:T(8,128)S(1)}, u32[]{:S(2)}, u32[]{:S(2)}) %collective-permute-start) | collective-permute-done | bytes 720928 | tf_op jit(solution)/shard_map/ppermute | solution.py:352
  140.8 1.9 dynamic-slice_add_fusion.2
  142.7 3.0 %collective-permute-start.3 = (f32[44,8,128]{2,1,0:T(8,128)}, f32[44,8,128]{2,1,0:T(8,128)S(1)}, u32[]{:S(2)}, u32[]{:S(2)}) collective-permute-start(f32[44,8,128]{2,1,0:T(8,128)} %get-tuple-element.34), channel_id=1, source_target_pairs={{0,96},{32,0},{64,32},{96,64},{1,97},{33,1},{65,33},{97,65},{2,98}... | collective-permute-start | bytes 540680 | tf_op jit(solution)/shard_map/ppermute | solution.py:323
  147.4 6.7 %collective-permute-done.3 = f32[44,8,128]{2,1,0:T(8,128)S(1)} collective-permute-done((f32[44,8,128]{2,1,0:T(8,128)}, f32[44,8,128]{2,1,0:T(8,128)S(1)}, u32[]{:S(2)}, u32[]{:S(2)}) %collective-permute-start.3) | collective-permute-done | bytes 180256 | tf_op jit(solution)/shard_map/ppermute | solution.py:323
  155.1 2.7 %collective-permute-done.1 = f32[44,8,128]{2,1,0:T(8,128)} collective-permute-done((f32[44,8,128]{2,1,0:T(8,128)}, f32[44,8,128]{2,1,0:T(8,128)}, u32[]{:S(2)}, u32[]{:S(2)}) %collective-permute-start.1) | collective-permute-done | bytes 180256 | tf_op jit(solution)/shard_map/ppermute | solution.py:323
  159.0 2.8 %collective-permute-start.6 = (f32[11,8,128]{2,1,0:T(8,128)S(1)}, f32[11,8,128]{2,1,0:T(8,128)S(1)}, u32[]{:S(2)}, u32[]{:S(2)}) collective-permute-start(f32[11,8,128]{2,1,0:T(8,128)S(1)} %get-tuple-element.39), channel_id=1, source_target_pairs={{0,3},{1,0},{2,1},{3,2},{4,7},{5,4},{6,5},{7,6},{8,11},{9,8},{10,9... | collective-permute-start | bytes 135176 | tf_op jit(solution)/shard_map/ppermute | solution.py:323
  163.5 2.1 collective-permute-done.6
  165.6 1.8 collective-permute-done.5
  167.9 4.7 %collective-permute-start.7 = (f32[11,8,128]{2,1,0:T(8,128)S(1)}, f32[11,8,128]{2,1,0:T(8,128)S(1)}, u32[]{:S(2)}, u32[]{:S(2)}) collective-permute-start(f32[11,8,128]{2,1,0:T(8,128)S(1)} %add_add_fusion.1), channel_id=1, source_target_pairs={{0,128},{128,0},{1,129},{129,1},{2,130},{130,2},{3,131},{131,3},{4... | collective-permute-start | bytes 135176 | tf_op jit(solution)/shard_map/ppermute | solution.py:352
  172.6 3.9 %collective-permute-done.7 = f32[11,8,128]{2,1,0:T(8,128)S(1)} collective-permute-done((f32[11,8,128]{2,1,0:T(8,128)S(1)}, f32[11,8,128]{2,1,0:T(8,128)S(1)}, u32[]{:S(2)}, u32[]{:S(2)}) %collective-permute-start.7) | collective-permute-done | bytes 45088 | tf_op jit(solution)/shard_map/ppermute | solution.py:352
  176.5 4.5 %collective-permute-start.10 = (f32[11,8,128]{2,1,0:T(8,128)S(1)}, f32[11,8,128]{2,1,0:T(8,128)S(1)}, u32[]{:S(2)}, u32[]{:S(2)}) collective-permute-start(f32[11,8,128]{2,1,0:T(8,128)S(1)} %add_multiply_fusion), channel_id=1, source_target_pairs={{0,12},{4,0},{8,4},{12,8},{1,13},{5,1},{9,5},{13,9},{2,14},{6,2},{... | collective-permute-start | bytes 135176 | tf_op jit(solution)/shard_map/ppermute | solution.py:323
  181.0 1.8 collective-permute-start.9
  186.9 6.1 %all-to-all-start.2 = ((bf16[16,2,6,16,256]{4,3,2,1,0:T(8,128)(2,1)}), bf16[16,2,6,16,256]{4,3,2,1,0:T(8,128)(2,1)}, u32[]{:S(2)}, u32[]{:S(2)}) async-start(bf16[16,2,6,16,256]{4,3,2,1,0:T(8,128)(2,1)} %get-tuple-element.23), calls=%async_computation.2 | async-start | bytes 3145728 | tf_op jit(solution)/shard_map/all_to_all | solution.py:410
  194.5 2.7 %collective-permute-start.12 = (f32[11,8,128]{2,1,0:T(8,128)S(1)}, f32[11,8,128]{2,1,0:T(8,128)S(1)}, u32[]{:S(2)}, u32[]{:S(2)}) collective-permute-start(f32[11,8,128]{2,1,0:T(8,128)S(1)} %add_bitcast_fusion), channel_id=1, source_target_pairs={{0,2},{1,3},{2,0},{3,1},{4,6},{5,7},{6,4},{7,5},{8,10},{9,11},{10,... | collective-permute-start | bytes 135176 | tf_op jit(solution)/shard_map/ppermute | solution.py:323
  198.6 3.4 %collective-permute-done.11 = f32[11,8,128]{2,1,0:T(8,128)S(1)} collective-permute-done((f32[11,8,128]{2,1,0:T(8,128)S(1)}, f32[11,8,128]{2,1,0:T(8,128)S(1)}, u32[]{:S(2)}, u32[]{:S(2)}) %collective-permute-start.11) | collective-permute-done | bytes 45088 | tf_op jit(solution)/shard_map/ppermute | solution.py:323
  202.3 2.6 %collective-permute-start.15 = (f32[44,8,128]{2,1,0:T(8,128)S(1)}, f32[44,8,128]{2,1,0:T(8,128)S(1)}, u32[]{:S(2)}, u32[]{:S(2)}) collective-permute-start(f32[44,8,128]{2,1,0:T(8,128)S(1)} %constant_dynamic-update-slice_fusion.3), channel_id=1, source_target_pairs={{0,64},{32,96},{64,0},{96,32},{1,65},{33,97},{65,1},{97,33},{2,66}... | collective-permute-start | bytes 540680 | tf_op jit(solution)/shard_map/ppermute | solution.py:323
  204.9 2.5 %collective-permute-start.16 = (f32[44,8,128]{2,1,0:T(8,128)S(1)}, f32[44,8,128]{2,1,0:T(8,128)S(1)}, u32[]{:S(2)}, u32[]{:S(2)}) collective-permute-start(f32[44,8,128]{2,1,0:T(8,128)S(1)} %constant_dynamic-update-slice_fusion.3), channel_id=1, source_target_pairs={{0,96},{32,0},{64,32},{96,64},{1,97},{33,1},{65,33},{97,65},{2,98}... | collective-permute-start | bytes 540680 | tf_op jit(solution)/shard_map/ppermute | solution.py:323
  207.5 4.2 %collective-permute-done.14 = f32[44,8,128]{2,1,0:T(8,128)S(1)} collective-permute-done((f32[44,8,128]{2,1,0:T(8,128)S(1)}, f32[44,8,128]{2,1,0:T(8,128)S(1)}, u32[]{:S(2)}, u32[]{:S(2)}) %collective-permute-start.14) | collective-permute-done | bytes 180256 | tf_op jit(solution)/shard_map/ppermute | solution.py:323
  211.9 2.2 collective-permute-done.17.other_ref
  215.2 3.3 %shard_map.150 = (bf16[2,8,256,256]{3,2,1,0:T(8,128)(2,1)}, bf16[2,8,256,256]{3,2,1,0:T(8,128)(2,1)}) custom-call(bf16[16,2,10,16,256]{4,3,2,1,0:T(8,128)(2,1)S(1)} %all-to-all-done.3.refs_0_), custom_call_target="tpu_custom_call" | custom-call | bytes 10485760 | tf_op jit(solution)/shard_map/pallas_call | solution.py:93
  218.5 8.6 %all-to-all-done.2.refs_0_ = bf16[16,2,6,16,256]{4,3,2,1,0:T(8,128)(2,1)} async-done(((bf16[16,2,6,16,256]{4,3,2,1,0:T(8,128)(2,1)}), bf16[16,2,6,16,256]{4,3,2,1,0:T(8,128)(2,1)}, u32[]{:S(2)}, u32[]{:S(2)}) %all-to-all-start.2) | async-done | bytes 1572896 | tf_op jit(solution)/shard_map/all_to_all | solution.py:410
  227.2 3.7 %shard_map.151 = (bf16[2,8,256,256]{3,2,1,0:T(8,128)(2,1)}, bf16[2,8,256,256]{3,2,1,0:T(8,128)(2,1)}) custom-call(bf16[16,2,6,16,256]{4,3,2,1,0:T(8,128)(2,1)} %all-to-all-done.2.refs_0_, bf16[2,8,256,256]{3,2,1,0:T(8,128)(2,1)} %get-tuple-element.25.refs_1_, ...), custom_call_target="tpu_custom_call", output_to_operand_aliasing={{0}: (1, {}), {1}: (2, {})} | custom-call | bytes 6291456 | tf_op jit(solution)/shard_map/pallas_call | solution.py:93
  (66 shorter events, 18.4 us)
Async XLA Ops:
  5.9 66.5 %all-to-all-start.1 = ((bf16[16,2,10,16,256]{4,3,2,1,0:T(8,128)(2,1)}), bf16[16,2,10,16,256]{4,3,2,1,0:T(8,128)(2,1)S(1)}, u32[]{:S(2)}, u32[]{:S(2)}) async-start(bf16[16,2,10,16,256]{4,3,2,1,0:T(8,128)(2,1)} %shard_map.147), calls=%async_computation.1 | async-start | bytes 5242880 | tf_op jit(solution)/shard_map/all_to_all | solution.py:410
  14.4 3.9 %copy-start.2 = (bf16[256,256]{1,0:T(8,128)(2,1)S(1)}, bf16[256,256]{1,0:T(8,128)(2,1)}, u32[]{:S(2)}) copy-start(bf16[256,256]{1,0:T(8,128)(2,1)} %param.16) | copy-start | bytes 393220
  14.4 4.0 %copy-start.3 = (bf16[256,256]{1,0:T(8,128)(2,1)S(1)}, bf16[256,256]{1,0:T(8,128)(2,1)}, u32[]{:S(2)}) copy-start(bf16[256,256]{1,0:T(8,128)(2,1)} %param.15) | copy-start | bytes 393220
  14.4 4.1 %copy-start.4 = (bf16[256,256]{1,0:T(8,128)(2,1)S(1)}, bf16[256,256]{1,0:T(8,128)(2,1)}, u32[]{:S(2)}) copy-start(bf16[256,256]{1,0:T(8,128)(2,1)} %param.14) | copy-start | bytes 393220
  14.5 4.2 %copy-start.5 = (bf16[256,256]{1,0:T(8,128)(2,1)S(1)}, bf16[256,256]{1,0:T(8,128)(2,1)}, u32[]{:S(2)}) copy-start(bf16[256,256]{1,0:T(8,128)(2,1)} %param.13) | copy-start | bytes 393220
  18.3 4.0 %copy-start.7 = (f32[256]{0:T(256)S(1)}, f32[256]{0:T(256)}, u32[]{:S(2)}) copy-start(f32[256]{0:T(256)} %param.21) | copy-start | bytes 3076
  18.3 4.0 %copy-start.8 = (f32[256]{0:T(256)S(1)}, f32[256]{0:T(256)}, u32[]{:S(2)}) copy-start(f32[256]{0:T(256)} %param.20) | copy-start | bytes 3076
  18.3 4.0 %copy-start.9 = (f32[256]{0:T(256)S(1)}, f32[256]{0:T(256)}, u32[]{:S(2)}) copy-start(f32[256]{0:T(256)} %param.19) | copy-start | bytes 3076
  21.2 57.9 %copy-start.6 = (f32[256]{0:T(256)S(1)}, f32[256]{0:T(256)}, u32[]{:S(2)}) copy-start(f32[256]{0:T(256)} %param.17) | copy-start | bytes 3076
  72.4 7.4 %copy-start = (bf16[16,2,10,16,256]{4,3,2,1,0:T(8,128)(2,1)}, bf16[16,2,10,16,256]{4,3,2,1,0:T(8,128)(2,1)S(1)}, u32[]{:S(2)}) copy-start(bf16[16,2,10,16,256]{4,3,2,1,0:T(8,128)(2,1)S(1)} %all-to-all-done.1.refs_1_.refs_2_) | copy-start | bytes 7864324
  72.4 42.7 %all-to-all-start = ((bf16[16,2,6,16,256]{4,3,2,1,0:T(8,128)(2,1)}), bf16[16,2,6,16,256]{4,3,2,1,0:T(8,128)(2,1)}, u32[]{:S(2)}, u32[]{:S(2)}) async-start(bf16[16,2,6,16,256]{4,3,2,1,0:T(8,128)(2,1)} %shard_map.146), calls=%async_computation | async-start | bytes 3145728 | tf_op jit(solution)/shard_map/all_to_all | solution.py:410
  115.1 71.8 %all-to-all-start.3 = ((bf16[16,2,10,16,256]{4,3,2,1,0:T(8,128)(2,1)}), bf16[16,2,10,16,256]{4,3,2,1,0:T(8,128)(2,1)S(1)}, u32[]{:S(2)}, u32[]{:S(2)}) async-start(bf16[16,2,10,16,256]{4,3,2,1,0:T(8,128)(2,1)} %get-tuple-element.24), calls=%async_computation.3 | async-start | bytes 5242880 | tf_op jit(solution)/shard_map/all_to_all | solution.py:410
  138.3 2.5 %collective-permute-start = (f32[176,8,128]{2,1,0:T(8,128)}, f32[176,8,128]{2,1,0:T(8,128)S(1)}, u32[]{:S(2)}, u32[]{:S(2)}) collective-permute-start(f32[176,8,128]{2,1,0:T(8,128)} %get-tuple-element.21), channel_id=1, source_target_pairs={{0,16},{16,0},{1,17},{17,1},{2,18},{18,2},{3,19},{19,3},{4,20},{20... | collective-permute-start | bytes 2162696 | tf_op jit(solution)/shard_map/ppermute | solution.py:352
  142.7 11.3 %collective-permute-start.3 = (f32[44,8,128]{2,1,0:T(8,128)}, f32[44,8,128]{2,1,0:T(8,128)S(1)}, u32[]{:S(2)}, u32[]{:S(2)}) collective-permute-start(f32[44,8,128]{2,1,0:T(8,128)} %get-tuple-element.34), channel_id=1, source_target_pairs={{0,96},{32,0},{64,32},{96,64},{1,97},{33,1},{65,33},{97,65},{2,98}... | collective-permute-start | bytes 540680 | tf_op jit(solution)/shard_map/ppermute | solution.py:323
  145.7 9.3 %collective-permute-start.2 = (f32[44,8,128]{2,1,0:T(8,128)}, f32[44,8,128]{2,1,0:T(8,128)}, u32[]{:S(2)}, u32[]{:S(2)}) collective-permute-start(f32[44,8,128]{2,1,0:T(8,128)} %get-tuple-element.35), channel_id=1, source_target_pairs={{0,64},{32,96},{64,0},{96,32},{1,65},{33,97},{65,1},{97,33},{2,66}... | collective-permute-start | bytes 540680 | tf_op jit(solution)/shard_map/ppermute | solution.py:323
  146.4 11.4 %collective-permute-start.1 = (f32[44,8,128]{2,1,0:T(8,128)}, f32[44,8,128]{2,1,0:T(8,128)}, u32[]{:S(2)}, u32[]{:S(2)}) collective-permute-start(f32[44,8,128]{2,1,0:T(8,128)} %get-tuple-element.33), channel_id=1, source_target_pairs={{0,32},{32,64},{64,96},{96,0},{1,33},{33,65},{65,97},{97,1},{2,34}... | collective-permute-start | bytes 540680 | tf_op jit(solution)/shard_map/ppermute | solution.py:323
  154.0 1.0 copy-start.1
  159.0 6.5 %collective-permute-start.6 = (f32[11,8,128]{2,1,0:T(8,128)S(1)}, f32[11,8,128]{2,1,0:T(8,128)S(1)}, u32[]{:S(2)}, u32[]{:S(2)}) collective-permute-start(f32[11,8,128]{2,1,0:T(8,128)S(1)} %get-tuple-element.39), channel_id=1, source_target_pairs={{0,3},{1,0},{2,1},{3,2},{4,7},{5,4},{6,5},{7,6},{8,11},{9,8},{10,9... | collective-permute-start | bytes 135176 | tf_op jit(solution)/shard_map/ppermute | solution.py:323
  161.8 5.6 %collective-permute-start.5 = (f32[11,8,128]{2,1,0:T(8,128)S(1)}, f32[11,8,128]{2,1,0:T(8,128)S(1)}, u32[]{:S(2)}, u32[]{:S(2)}) collective-permute-start(f32[11,8,128]{2,1,0:T(8,128)S(1)} %get-tuple-element.40), channel_id=1, source_target_pairs={{0,2},{1,3},{2,0},{3,1},{4,6},{5,7},{6,4},{7,5},{8,10},{9,11},{10,... | collective-permute-start | bytes 135176 | tf_op jit(solution)/shard_map/ppermute | solution.py:323
  162.6 5.3 %collective-permute-start.4 = (f32[11,8,128]{2,1,0:T(8,128)S(1)}, f32[11,8,128]{2,1,0:T(8,128)S(1)}, u32[]{:S(2)}, u32[]{:S(2)}) collective-permute-start(f32[11,8,128]{2,1,0:T(8,128)S(1)} %get-tuple-element.38), channel_id=1, source_target_pairs={{0,1},{1,2},{2,3},{3,0},{4,5},{5,6},{6,7},{7,4},{8,9},{9,10},{10,1... | collective-permute-start | bytes 135176 | tf_op jit(solution)/shard_map/ppermute | solution.py:323
  167.9 8.6 %collective-permute-start.7 = (f32[11,8,128]{2,1,0:T(8,128)S(1)}, f32[11,8,128]{2,1,0:T(8,128)S(1)}, u32[]{:S(2)}, u32[]{:S(2)}) collective-permute-start(f32[11,8,128]{2,1,0:T(8,128)S(1)} %add_add_fusion.1), channel_id=1, source_target_pairs={{0,128},{128,0},{1,129},{129,1},{2,130},{130,2},{3,131},{131,3},{4... | collective-permute-start | bytes 135176 | tf_op jit(solution)/shard_map/ppermute | solution.py:352
  176.5 7.9 %collective-permute-start.10 = (f32[11,8,128]{2,1,0:T(8,128)S(1)}, f32[11,8,128]{2,1,0:T(8,128)S(1)}, u32[]{:S(2)}, u32[]{:S(2)}) collective-permute-start(f32[11,8,128]{2,1,0:T(8,128)S(1)} %add_multiply_fusion), channel_id=1, source_target_pairs={{0,12},{4,0},{8,4},{12,8},{1,13},{5,1},{9,5},{13,9},{2,14},{6,2},{... | collective-permute-start | bytes 135176 | tf_op jit(solution)/shard_map/ppermute | solution.py:323
  181.0 4.9 %collective-permute-start.9 = (f32[11,8,128]{2,1,0:T(8,128)S(1)}, f32[11,8,128]{2,1,0:T(8,128)S(1)}, u32[]{:S(2)}, u32[]{:S(2)}) collective-permute-start(f32[11,8,128]{2,1,0:T(8,128)S(1)} %add_multiply_fusion), channel_id=1, source_target_pairs={{0,8},{4,12},{8,0},{12,4},{1,9},{5,13},{9,1},{13,5},{2,10},{6,14},... | collective-permute-start | bytes 135176 | tf_op jit(solution)/shard_map/ppermute | solution.py:323
  182.8 4.0 %collective-permute-start.8 = (f32[11,8,128]{2,1,0:T(8,128)S(1)}, f32[11,8,128]{2,1,0:T(8,128)S(1)}, u32[]{:S(2)}, u32[]{:S(2)}) collective-permute-start(f32[11,8,128]{2,1,0:T(8,128)S(1)} %add_multiply_fusion), channel_id=1, source_target_pairs={{0,4},{4,8},{8,12},{12,0},{1,5},{5,9},{9,13},{13,1},{2,6},{6,10},{... | collective-permute-start | bytes 135176 | tf_op jit(solution)/shard_map/ppermute | solution.py:323
  186.9 40.2 %all-to-all-start.2 = ((bf16[16,2,6,16,256]{4,3,2,1,0:T(8,128)(2,1)}), bf16[16,2,6,16,256]{4,3,2,1,0:T(8,128)(2,1)}, u32[]{:S(2)}, u32[]{:S(2)}) async-start(bf16[16,2,6,16,256]{4,3,2,1,0:T(8,128)(2,1)} %get-tuple-element.23), calls=%async_computation.2 | async-start | bytes 3145728 | tf_op jit(solution)/shard_map/all_to_all | solution.py:410
  193.0 9.1 %collective-permute-start.11 = (f32[11,8,128]{2,1,0:T(8,128)S(1)}, f32[11,8,128]{2,1,0:T(8,128)S(1)}, u32[]{:S(2)}, u32[]{:S(2)}) collective-permute-start(f32[11,8,128]{2,1,0:T(8,128)S(1)} %add_bitcast_fusion), channel_id=1, source_target_pairs={{0,1},{1,2},{2,3},{3,0},{4,5},{5,6},{6,7},{7,4},{8,9},{9,10},{10,1... | collective-permute-start | bytes 135176 | tf_op jit(solution)/shard_map/ppermute | solution.py:323
  194.5 7.6 %collective-permute-start.12 = (f32[11,8,128]{2,1,0:T(8,128)S(1)}, f32[11,8,128]{2,1,0:T(8,128)S(1)}, u32[]{:S(2)}, u32[]{:S(2)}) collective-permute-start(f32[11,8,128]{2,1,0:T(8,128)S(1)} %add_bitcast_fusion), channel_id=1, source_target_pairs={{0,2},{1,3},{2,0},{3,1},{4,6},{5,7},{6,4},{7,5},{8,10},{9,11},{10,... | collective-permute-start | bytes 135176 | tf_op jit(solution)/shard_map/ppermute | solution.py:323
  197.2 5.0 %collective-permute-start.13 = (f32[11,8,128]{2,1,0:T(8,128)S(1)}, f32[11,8,128]{2,1,0:T(8,128)S(1)}, u32[]{:S(2)}, u32[]{:S(2)}) collective-permute-start(f32[11,8,128]{2,1,0:T(8,128)S(1)} %add_bitcast_fusion), channel_id=1, source_target_pairs={{0,3},{1,0},{2,1},{3,2},{4,7},{5,4},{6,5},{7,6},{8,11},{9,8},{10,9... | collective-permute-start | bytes 135176 | tf_op jit(solution)/shard_map/ppermute | solution.py:323
  202.2 9.5 %collective-permute-start.14 = (f32[44,8,128]{2,1,0:T(8,128)S(1)}, f32[44,8,128]{2,1,0:T(8,128)S(1)}, u32[]{:S(2)}, u32[]{:S(2)}) collective-permute-start(f32[44,8,128]{2,1,0:T(8,128)S(1)} %constant_dynamic-update-slice_fusion.3), channel_id=1, source_target_pairs={{0,32},{32,64},{64,96},{96,0},{1,33},{33,65},{65,97},{97,1},{2,34}... | collective-permute-start | bytes 540680 | tf_op jit(solution)/shard_map/ppermute | solution.py:323
  202.3 9.4 %collective-permute-start.15 = (f32[44,8,128]{2,1,0:T(8,128)S(1)}, f32[44,8,128]{2,1,0:T(8,128)S(1)}, u32[]{:S(2)}, u32[]{:S(2)}) collective-permute-start(f32[44,8,128]{2,1,0:T(8,128)S(1)} %constant_dynamic-update-slice_fusion.3), channel_id=1, source_target_pairs={{0,64},{32,96},{64,0},{96,32},{1,65},{33,97},{65,1},{97,33},{2,66}... | collective-permute-start | bytes 540680 | tf_op jit(solution)/shard_map/ppermute | solution.py:323
  204.9 6.8 %collective-permute-start.16 = (f32[44,8,128]{2,1,0:T(8,128)S(1)}, f32[44,8,128]{2,1,0:T(8,128)S(1)}, u32[]{:S(2)}, u32[]{:S(2)}) collective-permute-start(f32[44,8,128]{2,1,0:T(8,128)S(1)} %constant_dynamic-update-slice_fusion.3), channel_id=1, source_target_pairs={{0,96},{32,0},{64,32},{96,64},{1,97},{33,1},{65,33},{97,65},{2,98}... | collective-permute-start | bytes 540680 | tf_op jit(solution)/shard_map/ppermute | solution.py:323
  211.8 2.3 collective-permute-start.17
where the time goes:
time: 232 us; the launch traced here: 231 us
  waiting for transfers between devices  102 us (44%)
  Pallas kernels  61 us (26%)
  starting transfers between devices  57.9 us (25%)
  other arithmetic  5.63 us (2%)
  local copies, waits for them, and re-layouts  3.19 us (1%)
    all_to_all x4, waiting for transfers between devices, exchange(): return lax.all_to_all(value, DAP, 0, 0, tiled=True)  67.4 us
    pallas_call x2, Pallas kernels, columns(): pl.pallas_call(functools.partial(pair_kernel, STEPS, sums is not None, la...  43.7 us
    all_to_all x4, starting transfers between devices, exchange(): return lax.all_to_all(value, DAP, 0, 0, tiled=True)  26.7 us
    ppermute x15, waiting for transfers between devices, shift(): lax.ppermute(value, axes, [(k, (k + step) % size) for k in range(size)])  26.5 us
    ppermute x15, starting transfers between devices, shift(): lax.ppermute(value, axes, [(k, (k + step) % size) for k in range(size)])  26.3 us
    pallas_call x2, Pallas kernels, pack(): pl.pallas_call(pack_kernel, grid=(units, MEMBERS // GROUP), in_specs=[row...  9.12 us
    ppermute x3, waiting for transfers between devices, swap(): return lax.ppermute(value, axis, [(0, 1), (1, 0)])  8.4 us
    pallas_call x2, Pallas kernels, unpack(): pl.pallas_call(unpack_kernel, grid=(units, MEMBERS // GROUP), in_specs=[b...  7.04 us
  transfers between devices with their start and end apart: 22, of which 17 were waited for; matrix products, arithmetic and copies ran while one was open for 4% of the time, Pallas kernels for 23%

commit v1 on v0

--- a/solution.py
+++ b/solution.py
@@ -26,13 +26,11 @@
 OWN_ROWS = ROWS // MEMBERS
 UNITS = 4
 PAIRS = 2
-STEPS = 2
 DAP = ("z_lo", "x")
 BATCH = ("z_hi", "y", "core")
 RING = ("z_hi", "z_lo")
 TILES = 176
-GROUP = 16
-COUNT = GROUP * 2 * PAIRS
+COUNT = MEMBERS * 2 * PAIRS
 VMEM = 60 * 2**20
 
 
@@ -42,64 +40,92 @@
     )
 
 
-def unit_specs(first):
-    rows = pl.BlockSpec(
-        (1, OWN_ROWS, COUNT, C),
-        lambda n, g: ((first + n) // UNITS, 0, (first + n) % UNITS * (MEMBERS // GROUP) + g, 0),
-    )
-    packed = pl.BlockSpec((GROUP, 2, PAIRS, 16, C), lambda n, g: (g, 0, n, 0, 0))
-    return rows, packed
-
-
-def pack_kernel(x_ref, cot_ref, out_ref, wide):
-    for which, ref in enumerate((x_ref, cot_ref)):
-        for side in range(2):
-            lanes = slice(side * 128, side * 128 + 128)
-            for row in range(OWN_ROWS):
-                wide[which, side, pl.ds(row, COUNT, stride=OWN_ROWS), :] = ref[0, row, :, lanes].astype(F32)
-            out_ref[:, which, :, :, lanes] = wide[which, side].reshape(GROUP, PAIRS, 16, 128).astype(BF16)
+def rows_of(ref, unit):
+    return ref.at[unit // UNITS, :, pl.ds(unit % UNITS * COUNT, COUNT), :]
+
+
+def pack_kernel(first, units, x_ref, cot_ref, out_ref, held, made, in_sems, out_sems):
+    def arrival(n, which):
+        source = rows_of((x_ref, cot_ref)[which], first + n)
+        return pltpu.make_async_copy(source, held.at[n, which], in_sems.at[n, which])
+
+    def departure(n):
+        target = out_ref.at[:, :, pl.ds(n * PAIRS, PAIRS), :, :]
+        return pltpu.make_async_copy(made.at[n], target, out_sems.at[n])
+
+    for n in range(units):
+        for which in range(2):
+            arrival(n, which).start()
+    for n in range(units):
+        for which in range(2):
+            arrival(n, which).wait()
+            turned = jnp.swapaxes(held[n, which], 0, 1)
+            made[n, :, which] = turned.reshape(MEMBERS, PAIRS, 16, C)
+        departure(n).start()
+    for n in range(units):
+        departure(n).wait()
 
 
 def pack(alignment, cotangent, first, units):
-    rows, packed = unit_specs(first)
+    anywhere = pl.BlockSpec(memory_space=pl.ANY)
     return pl.pallas_call(
-        pack_kernel,
-        grid=(units, MEMBERS // GROUP),
-        in_specs=[rows, rows],
-        out_specs=packed,
+        functools.partial(pack_kernel, first, units),
+        in_specs=[anywhere, anywhere],
+        out_specs=anywhere,
         out_shape=pltpu.HBM((MEMBERS, 2, units * PAIRS, 16, C), BF16),
-        scratch_shapes=[pltpu.VMEM((2, 2, COUNT * OWN_ROWS, 128), F32)],
+        scratch_shapes=[
+            pltpu.VMEM((units, 2, OWN_ROWS, COUNT, C), BF16),
+            pltpu.VMEM((units, MEMBERS, 2, PAIRS, 16, C), BF16),
+            pltpu.SemaphoreType.DMA((units, 2)),
+            pltpu.SemaphoreType.DMA((units,)),
+        ],
         compiler_params=pltpu.CompilerParams(vmem_limit_bytes=VMEM),
-        cost_estimate=pl.CostEstimate(flops=0, bytes_accessed=units * 2**21, transcendentals=0),
+        cost_estimate=pl.CostEstimate(flops=0, bytes_accessed=units * 2**20, transcendentals=0),
     )(alignment, cotangent)
 
 
-def unpack_kernel(*refs):
-    in_ref, upd_ref, grad_ref, wide = refs[0], *refs[-3:]
-    for which, ref in enumerate((upd_ref, grad_ref)):
-        for side in range(2):
-            lanes = slice(side * 128, side * 128 + 128)
-            wide[which, side] = in_ref[:, which, :, :, lanes].astype(F32).reshape(COUNT * OWN_ROWS, 128)
-            for row in range(OWN_ROWS):
-                ref[0, row, :, lanes] = wide[
-                    which, side, pl.ds(row, COUNT, stride=OWN_ROWS), :
-                ].astype(BF16)
+def unpack_kernel(first, units, *refs):
+    in_ref, upd_ref, grad_ref, held, made, in_sems, out_sems = refs[0], *refs[-6:]
+
+    def arrival(n):
+        source = in_ref.at[:, :, pl.ds(n * PAIRS, PAIRS), :, :]
+        return pltpu.make_async_copy(source, held.at[n], in_sems.at[n])
+
+    def departure(n, which):
+        target = rows_of((upd_ref, grad_ref)[which], first + n)
+        return pltpu.make_async_copy(made.at[n, which], target, out_sems.at[n, which])
+
+    for n in range(units):
+        arrival(n).start()
+    for n in range(units):
+        arrival(n).wait()
+        for which in range(2):
+            turned = held[n, :, which].reshape(COUNT, OWN_ROWS, C)
+            made[n, which] = jnp.swapaxes(turned, 0, 1)
+            departure(n, which).start()
+    for n in range(units):
+        for which in range(2):
+            departure(n, which).wait()
 
 
 def unpack(packed, first, structs, earlier):
-    rows, blocks = unit_specs(first)
+    anywhere = pl.BlockSpec(memory_space=pl.ANY)
     shape = pltpu.HBM((structs, OWN_ROWS, RES, C), BF16)
     units = packed.shape[2] // PAIRS
     return pl.pallas_call(
-        unpack_kernel,
-        grid=(units, MEMBERS // GROUP),
-        in_specs=[blocks] + [pl.BlockSpec(memory_space=pl.ANY)] * len(earlier),
-        out_specs=[rows, rows],
+        functools.partial(unpack_kernel, first, units),
+        in_specs=[anywhere] * (1 + len(earlier)),
+        out_specs=[anywhere, anywhere],
         out_shape=[shape, shape],
         input_output_aliases={1 + k: k for k in range(len(earlier))},
-        scratch_shapes=[pltpu.VMEM((2, 2, COUNT * OWN_ROWS, 128), F32)],
+        scratch_shapes=[
+            pltpu.VMEM((units, MEMBERS, 2, PAIRS, 16, C), BF16),
+            pltpu.VMEM((units, 2, OWN_ROWS, COUNT, C), BF16),
+            pltpu.SemaphoreType.DMA((units,)),
+            pltpu.SemaphoreType.DMA((units, 2)),
+        ],
         compiler_params=pltpu.CompilerParams(vmem_limit_bytes=24 * 2**20),
-        cost_estimate=pl.CostEstimate(flops=0, bytes_accessed=units * 2**21, transcendentals=0),
+        cost_estimate=pl.CostEstimate(flops=0, bytes_accessed=units * 2**20, transcendentals=0),
     )(packed, *earlier)
 
 
@@ -270,8 +296,8 @@
             other_ref[...] = sums_ref[1 - core]
 
 
-def columns(packed, core, params, sums=None, last=False):
-    pairs = packed.shape[2] // STEPS
+def columns(packed, core, params, steps, sums=None, last=False):
+    pairs = packed.shape[2] // steps
 
     def part(which):
         return pl.BlockSpec((MEMBERS, 1, pairs, 16, C), lambda p: (0, which, p, 0, 0))
@@ -304,8 +330,8 @@
         out_specs.append(whole((2, *half)))
         out_shape.append(pltpu.HBM((2, *half), F32))
     return pl.pallas_call(
-        functools.partial(pair_kernel, STEPS, sums is not None, last),
-        grid=(STEPS,),
+        functools.partial(pair_kernel, steps, sums is not None, last),
+        grid=(steps,),
         in_specs=in_specs,
         out_specs=out_specs,
         out_shape=out_shape,
@@ -411,9 +437,9 @@
 
     first = exchange(pack(alignment, cotangent, 0, 5))
     second = exchange(pack(alignment, cotangent, 5, 3))
-    early, sums = columns(first, core, params)
+    early, sums = columns(first, core, params, 2)
     early = exchange(early)
-    late, own, other = columns(second, core, params, sums, last=True)
+    late, own, other = columns(second, core, params, 1, sums, last=True)
     tiles = rows_sum(own, other)
     tiles = (tiles + swap(tiles, "z_hi")) * FACTOR
     tiles, late = after((meet_sum(tiles, "z_lo", 4), late))

time: 232 us -> 230 us (level)
  Pallas kernels: 61 us -> 53.7 us
  waiting for transfers between devices: 102 us -> 106 us
    pallas_call x6, Pallas kernels: 59.8 us -> 52.5 us  [the longest x2 43.3 us: columns(): pl.pallas_call(functools.partial(pair_kernel, steps, sums is not None, la...]
    all_to_all x4, waiting for transfers between devices: 67.4 us -> 70.8 us  [exchange(): return lax.all_to_all(value, DAP, 0, 0, tiled=True)]
  transfers between devices with their start and end apart: 22 -> 22, of which waited for: 17 -> 19; matrix products, arithmetic and copies ran while one was open for 4% -> 4% of each run, Pallas kernels for 23% -> 21%
where the time goes in v1:
time: 230 us; the launch traced here: 227 us
  waiting for transfers between devices  106 us (46%)
  starting transfers between devices  57.8 us (25%)
  Pallas kernels  53.7 us (23%)
  other arithmetic  5.63 us (2%)
  local copies, waits for them, and re-layouts  3.19 us (1%)
    all_to_all x4, waiting for transfers between devices, exchange(): return lax.all_to_all(value, DAP, 0, 0, tiled=True)  70.8 us
    pallas_call x2, Pallas kernels, columns(): pl.pallas_call(functools.partial(pair_kernel, steps, sums is not None, la...  43.3 us
    all_to_all x4, starting transfers between devices, exchange(): return lax.all_to_all(value, DAP, 0, 0, tiled=True)  27.4 us
    ppermute x15, waiting for transfers between devices, shift(): lax.ppermute(value, axes, [(k, (k + step) % size) for k in range(size)])  26.6 us
    ppermute x15, starting transfers between devices, shift(): lax.ppermute(value, axes, [(k, (k + step) % size) for k in range(size)])  25.8 us
    ppermute x3, waiting for transfers between devices, swap(): return lax.ppermute(value, axis, [(0, 1), (1, 0)])  8.55 us
    pallas_call x2, Pallas kernels, pack(): pl.pallas_call(functools.partial(pack_kernel, first, units), in_specs=[an...  5.08 us
    ppermute x3, starting transfers between devices, swap(): return lax.ppermute(value, axis, [(0, 1), (1, 0)])  4.62 us
  transfers between devices with their start and end apart: 22, of which 19 were waited for; matrix products, arithmetic and copies ran while one was open for 4% of the time, Pallas kernels for 21%

profile of v1, /device:TPU:32, one launch (start us, length us, event | category | flops | bytes accessed | tf_op | source)
XLA Modules:
  0.0 227.4 jit_solution(788391094257346699)
XLA Ops:
  0.6 2.7 %shard_map.147 = bf16[16,2,10,16,256]{4,3,2,1,0:T(8,128)(2,1)} custom-call(bf16[2,8,256,256]{3,2,1,0:T(8,128)(2,1)} %x_ref.3, bf16[2,8,256,256]{3,2,1,0:T(8,128)(2,1)} %cot_ref.3), custom_call_target="tpu_custom_call" | custom-call | bytes 5242880 | tf_op jit(solution)/shard_map/pallas_call | solution.py:71
  3.3 8.5 %all-to-all-start.1 = ((bf16[16,2,10,16,256]{4,3,2,1,0:T(8,128)(2,1)}), bf16[16,2,10,16,256]{4,3,2,1,0:T(8,128)(2,1)S(1)}, u32[]{:S(2)}, u32[]{:S(2)}) async-start(bf16[16,2,10,16,256]{4,3,2,1,0:T(8,128)(2,1)} %shard_map.147), calls=%async_computation.1 | async-start | bytes 5242880 | tf_op jit(solution)/shard_map/all_to_all | solution.py:436
  11.9 2.4 %shard_map.146 = bf16[16,2,6,16,256]{4,3,2,1,0:T(8,128)(2,1)} custom-call(bf16[2,8,256,256]{3,2,1,0:T(8,128)(2,1)} %x_ref.3, bf16[2,8,256,256]{3,2,1,0:T(8,128)(2,1)} %cot_ref.3), custom_call_target="tpu_custom_call" | custom-call | bytes 3145728 | tf_op jit(solution)/shard_map/pallas_call | solution.py:71
  15.4 1.8 fusion
  19.0 50.8 %all-to-all-done.1.refs_1_.refs_2_ = bf16[16,2,10,16,256]{4,3,2,1,0:T(8,128)(2,1)S(1)} async-done(((bf16[16,2,10,16,256]{4,3,2,1,0:T(8,128)(2,1)}), bf16[16,2,10,16,256]{4,3,2,1,0:T(8,128)(2,1)S(1)}, u32[]{:S(2)}, u32[]{:S(2)}) %all-to-all-start.1) | async-done | bytes 2621472 | tf_op jit(solution)/shard_map/all_to_all | solution.py:436
  69.8 7.0 %all-to-all-start = ((bf16[16,2,6,16,256]{4,3,2,1,0:T(8,128)(2,1)}), bf16[16,2,6,16,256]{4,3,2,1,0:T(8,128)(2,1)}, u32[]{:S(2)}, u32[]{:S(2)}) async-start(bf16[16,2,6,16,256]{4,3,2,1,0:T(8,128)(2,1)} %shard_map.146), calls=%async_computation | async-start | bytes 3145728 | tf_op jit(solution)/shard_map/all_to_all | solution.py:436
  77.6 25.9 %shard_map.148 = (bf16[16,2,10,16,256]{4,3,2,1,0:T(8,128)(2,1)}, f32[2,176,8,128]{3,2,1,0:T(8,128)}) custom-call(s32[1]{0:T(128)} %bitcast.refs_0_.core_ref, bf16[16,2,10,16,256]{4,3,2,1,0:T(8,128)(2,1)} %copy-done, bf16[16,2,10,16,256]{4,3,2,1,0:T(8,128)(2,1)} %copy-done, bf16[256,1024]{1,0:T(8,128)(2,1)} %copy.23.refs_3_, ...), custom_call_target="tpu_custom_call" | custom-call | flops 40000000000 | bytes 8388608 | tf_op jit(solution)/shard_map/pallas_call | solution.py:332
  103.5 9.2 %all-to-all-done.refs_1_.refs_2_ = bf16[16,2,6,16,256]{4,3,2,1,0:T(8,128)(2,1)} async-done(((bf16[16,2,6,16,256]{4,3,2,1,0:T(8,128)(2,1)}), bf16[16,2,6,16,256]{4,3,2,1,0:T(8,128)(2,1)}, u32[]{:S(2)}, u32[]{:S(2)}) %all-to-all-start) | async-done | bytes 1572896 | tf_op jit(solution)/shard_map/all_to_all | solution.py:436
  112.7 5.8 %all-to-all-start.3 = ((bf16[16,2,10,16,256]{4,3,2,1,0:T(8,128)(2,1)}), bf16[16,2,10,16,256]{4,3,2,1,0:T(8,128)(2,1)S(1)}, u32[]{:S(2)}, u32[]{:S(2)}) async-start(bf16[16,2,10,16,256]{4,3,2,1,0:T(8,128)(2,1)} %get-tuple-element.24), calls=%async_computation.3 | async-start | bytes 5242880 | tf_op jit(solution)/shard_map/all_to_all | solution.py:436
  118.5 17.3 %shard_map.149 = (bf16[16,2,6,16,256]{4,3,2,1,0:T(8,128)(2,1)}, f32[176,8,128]{2,1,0:T(8,128)}, f32[176,8,128]{2,1,0:T(8,128)}) custom-call(s32[1]{0:T(128)} %bitcast.refs_0_.core_ref, bf16[16,2,6,16,256]{4,3,2,1,0:T(8,128)(2,1)} %all-to-all-done.refs_1_.refs_2_, bf16[16,2,6,16,256]{4,3,2,1,0:T(8,128)(2,1)} %all-to-all-done.refs_1_.refs_2_, ...), custom_call_target="tpu_custom_call" | custom-call | flops 24000000000 | bytes 8388608 | tf_op jit(solution)/shard_map/pallas_call | solution.py:332
  135.9 2.4 %collective-permute-done = f32[176,8,128]{2,1,0:T(8,128)S(1)} collective-permute-done((f32[176,8,128]{2,1,0:T(8,128)}, f32[176,8,128]{2,1,0:T(8,128)S(1)}, u32[]{:S(2)}, u32[]{:S(2)}) %collective-permute-start) | collective-permute-done | bytes 720928 | tf_op jit(solution)/shard_map/ppermute | solution.py:378
  138.3 1.9 dynamic-slice_add_fusion.2
  140.2 3.0 %collective-permute-start.3 = (f32[44,8,128]{2,1,0:T(8,128)}, f32[44,8,128]{2,1,0:T(8,128)S(1)}, u32[]{:S(2)}, u32[]{:S(2)}) collective-permute-start(f32[44,8,128]{2,1,0:T(8,128)} %get-tuple-element.34), channel_id=1, source_target_pairs={{0,96},{32,0},{64,32},{96,64},{1,97},{33,1},{65,33},{97,65},{2,98}... | collective-permute-start | bytes 540680 | tf_op jit(solution)/shard_map/ppermute | solution.py:349
  144.8 6.7 %collective-permute-done.3 = f32[44,8,128]{2,1,0:T(8,128)S(1)} collective-permute-done((f32[44,8,128]{2,1,0:T(8,128)}, f32[44,8,128]{2,1,0:T(8,128)S(1)}, u32[]{:S(2)}, u32[]{:S(2)}) %collective-permute-start.3) | collective-permute-done | bytes 180256 | tf_op jit(solution)/shard_map/ppermute | solution.py:349
  152.5 2.7 %collective-permute-done.1 = f32[44,8,128]{2,1,0:T(8,128)} collective-permute-done((f32[44,8,128]{2,1,0:T(8,128)}, f32[44,8,128]{2,1,0:T(8,128)}, u32[]{:S(2)}, u32[]{:S(2)}) %collective-permute-start.1) | collective-permute-done | bytes 180256 | tf_op jit(solution)/shard_map/ppermute | solution.py:349
  156.4 2.8 %collective-permute-start.6 = (f32[11,8,128]{2,1,0:T(8,128)S(1)}, f32[11,8,128]{2,1,0:T(8,128)S(1)}, u32[]{:S(2)}, u32[]{:S(2)}) collective-permute-start(f32[11,8,128]{2,1,0:T(8,128)S(1)} %get-tuple-element.39), channel_id=1, source_target_pairs={{0,3},{1,0},{2,1},{3,2},{4,7},{5,4},{6,5},{7,6},{8,11},{9,8},{10,9... | collective-permute-start | bytes 135176 | tf_op jit(solution)/shard_map/ppermute | solution.py:349
  160.9 2.2 collective-permute-done.6
  163.1 1.6 collective-permute-done.5
  165.3 4.5 %collective-permute-start.7 = (f32[11,8,128]{2,1,0:T(8,128)S(1)}, f32[11,8,128]{2,1,0:T(8,128)S(1)}, u32[]{:S(2)}, u32[]{:S(2)}) collective-permute-start(f32[11,8,128]{2,1,0:T(8,128)S(1)} %add_add_fusion.1), channel_id=1, source_target_pairs={{0,128},{128,0},{1,129},{129,1},{2,130},{130,2},{3,131},{131,3},{4... | collective-permute-start | bytes 135176 | tf_op jit(solution)/shard_map/ppermute | solution.py:378
  169.9 4.0 %collective-permute-done.7 = f32[11,8,128]{2,1,0:T(8,128)S(1)} collective-permute-done((f32[11,8,128]{2,1,0:T(8,128)S(1)}, f32[11,8,128]{2,1,0:T(8,128)S(1)}, u32[]{:S(2)}, u32[]{:S(2)}) %collective-permute-start.7) | collective-permute-done | bytes 45088 | tf_op jit(solution)/shard_map/ppermute | solution.py:378
  173.8 4.5 %collective-permute-start.10 = (f32[11,8,128]{2,1,0:T(8,128)S(1)}, f32[11,8,128]{2,1,0:T(8,128)S(1)}, u32[]{:S(2)}, u32[]{:S(2)}) collective-permute-start(f32[11,8,128]{2,1,0:T(8,128)S(1)} %add_multiply_fusion), channel_id=1, source_target_pairs={{0,12},{4,0},{8,4},{12,8},{1,13},{5,1},{9,5},{13,9},{2,14},{6,2},{... | collective-permute-start | bytes 135176 | tf_op jit(solution)/shard_map/ppermute | solution.py:349
  180.5 2.8 %collective-permute-done.9 = f32[11,8,128]{2,1,0:T(8,128)S(1)} collective-permute-done((f32[11,8,128]{2,1,0:T(8,128)S(1)}, f32[11,8,128]{2,1,0:T(8,128)S(1)}, u32[]{:S(2)}, u32[]{:S(2)}) %collective-permute-start.9) | collective-permute-done | bytes 45088 | tf_op jit(solution)/shard_map/ppermute | solution.py:349
  184.0 6.1 %all-to-all-start.2 = ((bf16[16,2,6,16,256]{4,3,2,1,0:T(8,128)(2,1)}), bf16[16,2,6,16,256]{4,3,2,1,0:T(8,128)(2,1)}, u32[]{:S(2)}, u32[]{:S(2)}) async-start(bf16[16,2,6,16,256]{4,3,2,1,0:T(8,128)(2,1)} %get-tuple-element.23), calls=%async_computation.2 | async-start | bytes 3145728 | tf_op jit(solution)/shard_map/all_to_all | solution.py:436
  191.6 2.7 %collective-permute-start.12 = (f32[11,8,128]{2,1,0:T(8,128)S(1)}, f32[11,8,128]{2,1,0:T(8,128)S(1)}, u32[]{:S(2)}, u32[]{:S(2)}) collective-permute-start(f32[11,8,128]{2,1,0:T(8,128)S(1)} %add_bitcast_fusion), channel_id=1, source_target_pairs={{0,2},{1,3},{2,0},{3,1},{4,6},{5,7},{6,4},{7,5},{8,10},{9,11},{10,... | collective-permute-start | bytes 135176 | tf_op jit(solution)/shard_map/ppermute | solution.py:349
  195.7 2.4 %collective-permute-done.11 = f32[11,8,128]{2,1,0:T(8,128)S(1)} collective-permute-done((f32[11,8,128]{2,1,0:T(8,128)S(1)}, f32[11,8,128]{2,1,0:T(8,128)S(1)}, u32[]{:S(2)}, u32[]{:S(2)}) %collective-permute-start.11) | collective-permute-done | bytes 45088 | tf_op jit(solution)/shard_map/ppermute | solution.py:349
  199.2 2.7 %collective-permute-start.15 = (f32[44,8,128]{2,1,0:T(8,128)S(1)}, f32[44,8,128]{2,1,0:T(8,128)S(1)}, u32[]{:S(2)}, u32[]{:S(2)}) collective-permute-start(f32[44,8,128]{2,1,0:T(8,128)S(1)} %constant_dynamic-update-slice_fusion.3), channel_id=1, source_target_pairs={{0,64},{32,96},{64,0},{96,32},{1,65},{33,97},{65,1},{97,33},{2,66}... | collective-permute-start | bytes 540680 | tf_op jit(solution)/shard_map/ppermute | solution.py:349
  201.8 2.4 %collective-permute-start.16 = (f32[44,8,128]{2,1,0:T(8,128)S(1)}, f32[44,8,128]{2,1,0:T(8,128)S(1)}, u32[]{:S(2)}, u32[]{:S(2)}) collective-permute-start(f32[44,8,128]{2,1,0:T(8,128)S(1)} %constant_dynamic-update-slice_fusion.3), channel_id=1, source_target_pairs={{0,96},{32,0},{64,32},{96,64},{1,97},{33,1},{65,33},{97,65},{2,98}... | collective-permute-start | bytes 540680 | tf_op jit(solution)/shard_map/ppermute | solution.py:349
  204.3 4.3 %collective-permute-done.14 = f32[44,8,128]{2,1,0:T(8,128)S(1)} collective-permute-done((f32[44,8,128]{2,1,0:T(8,128)S(1)}, f32[44,8,128]{2,1,0:T(8,128)S(1)}, u32[]{:S(2)}, u32[]{:S(2)}) %collective-permute-start.14) | collective-permute-done | bytes 180256 | tf_op jit(solution)/shard_map/ppermute | solution.py:349
  208.8 2.2 collective-permute-done.17.other_ref
  212.2 1.9 shard_map.150
  214.0 10.8 %all-to-all-done.2.refs_0_ = bf16[16,2,6,16,256]{4,3,2,1,0:T(8,128)(2,1)} async-done(((bf16[16,2,6,16,256]{4,3,2,1,0:T(8,128)(2,1)}), bf16[16,2,6,16,256]{4,3,2,1,0:T(8,128)(2,1)}, u32[]{:S(2)}, u32[]{:S(2)}) %all-to-all-start.2) | async-done | bytes 1572896 | tf_op jit(solution)/shard_map/all_to_all | solution.py:436
  224.9 2.3 %shard_map.151 = (bf16[2,8,256,256]{3,2,1,0:T(8,128)(2,1)}, bf16[2,8,256,256]{3,2,1,0:T(8,128)(2,1)}) custom-call(bf16[16,2,6,16,256]{4,3,2,1,0:T(8,128)(2,1)} %all-to-all-done.2.refs_0_, bf16[2,8,256,256]{3,2,1,0:T(8,128)(2,1)} %get-tuple-element.25.refs_1_, ...), custom_call_target="tpu_custom_call", output_to_operand_aliasing={{0}: (1, {}), {1}: (2, {})} | custom-call | bytes 3145728 | tf_op jit(solution)/shard_map/pallas_call | solution.py:115
  (66 shorter events, 18.1 us)
Async XLA Ops:
  3.3 66.5 %all-to-all-start.1 = ((bf16[16,2,10,16,256]{4,3,2,1,0:T(8,128)(2,1)}), bf16[16,2,10,16,256]{4,3,2,1,0:T(8,128)(2,1)S(1)}, u32[]{:S(2)}, u32[]{:S(2)}) async-start(bf16[16,2,10,16,256]{4,3,2,1,0:T(8,128)(2,1)} %shard_map.147), calls=%async_computation.1 | async-start | bytes 5242880 | tf_op jit(solution)/shard_map/all_to_all | solution.py:436
  11.8 2.5 %copy-start.2 = (bf16[256,256]{1,0:T(8,128)(2,1)S(1)}, bf16[256,256]{1,0:T(8,128)(2,1)}, u32[]{:S(2)}) copy-start(bf16[256,256]{1,0:T(8,128)(2,1)} %param.16) | copy-start | bytes 393220
  11.8 2.6 %copy-start.3 = (bf16[256,256]{1,0:T(8,128)(2,1)S(1)}, bf16[256,256]{1,0:T(8,128)(2,1)}, u32[]{:S(2)}) copy-start(bf16[256,256]{1,0:T(8,128)(2,1)} %param.15) | copy-start | bytes 393220
  11.9 2.7 %copy-start.4 = (bf16[256,256]{1,0:T(8,128)(2,1)S(1)}, bf16[256,256]{1,0:T(8,128)(2,1)}, u32[]{:S(2)}) copy-start(bf16[256,256]{1,0:T(8,128)(2,1)} %param.14) | copy-start | bytes 393220
  11.9 2.8 %copy-start.5 = (bf16[256,256]{1,0:T(8,128)(2,1)S(1)}, bf16[256,256]{1,0:T(8,128)(2,1)}, u32[]{:S(2)}) copy-start(bf16[256,256]{1,0:T(8,128)(2,1)} %param.13) | copy-start | bytes 393220
  14.3 4.1 %copy-start.7 = (f32[256]{0:T(256)S(1)}, f32[256]{0:T(256)}, u32[]{:S(2)}) copy-start(f32[256]{0:T(256)} %param.21) | copy-start | bytes 3076
  14.3 4.1 %copy-start.8 = (f32[256]{0:T(256)S(1)}, f32[256]{0:T(256)}, u32[]{:S(2)}) copy-start(f32[256]{0:T(256)} %param.20) | copy-start | bytes 3076
  14.3 4.0 %copy-start.9 = (f32[256]{0:T(256)S(1)}, f32[256]{0:T(256)}, u32[]{:S(2)}) copy-start(f32[256]{0:T(256)} %param.19) | copy-start | bytes 3076
  17.2 59.6 %copy-start.6 = (f32[256]{0:T(256)S(1)}, f32[256]{0:T(256)}, u32[]{:S(2)}) copy-start(f32[256]{0:T(256)} %param.17) | copy-start | bytes 3076
  69.8 7.8 %copy-start = (bf16[16,2,10,16,256]{4,3,2,1,0:T(8,128)(2,1)}, bf16[16,2,10,16,256]{4,3,2,1,0:T(8,128)(2,1)S(1)}, u32[]{:S(2)}) copy-start(bf16[16,2,10,16,256]{4,3,2,1,0:T(8,128)(2,1)S(1)} %all-to-all-done.1.refs_1_.refs_2_) | copy-start | bytes 7864324
  69.8 42.9 %all-to-all-start = ((bf16[16,2,6,16,256]{4,3,2,1,0:T(8,128)(2,1)}), bf16[16,2,6,16,256]{4,3,2,1,0:T(8,128)(2,1)}, u32[]{:S(2)}, u32[]{:S(2)}) async-start(bf16[16,2,6,16,256]{4,3,2,1,0:T(8,128)(2,1)} %shard_map.146), calls=%async_computation | async-start | bytes 3145728 | tf_op jit(solution)/shard_map/all_to_all | solution.py:436
  112.7 71.3 %all-to-all-start.3 = ((bf16[16,2,10,16,256]{4,3,2,1,0:T(8,128)(2,1)}), bf16[16,2,10,16,256]{4,3,2,1,0:T(8,128)(2,1)S(1)}, u32[]{:S(2)}, u32[]{:S(2)}) async-start(bf16[16,2,10,16,256]{4,3,2,1,0:T(8,128)(2,1)} %get-tuple-element.24), calls=%async_computation.3 | async-start | bytes 5242880 | tf_op jit(solution)/shard_map/all_to_all | solution.py:436
  135.9 2.4 %collective-permute-start = (f32[176,8,128]{2,1,0:T(8,128)}, f32[176,8,128]{2,1,0:T(8,128)S(1)}, u32[]{:S(2)}, u32[]{:S(2)}) collective-permute-start(f32[176,8,128]{2,1,0:T(8,128)} %get-tuple-element.21), channel_id=1, source_target_pairs={{0,16},{16,0},{1,17},{17,1},{2,18},{18,2},{3,19},{19,3},{4,20},{20... | collective-permute-start | bytes 2162696 | tf_op jit(solution)/shard_map/ppermute | solution.py:378
  140.2 11.3 %collective-permute-start.3 = (f32[44,8,128]{2,1,0:T(8,128)}, f32[44,8,128]{2,1,0:T(8,128)S(1)}, u32[]{:S(2)}, u32[]{:S(2)}) collective-permute-start(f32[44,8,128]{2,1,0:T(8,128)} %get-tuple-element.34), channel_id=1, source_target_pairs={{0,96},{32,0},{64,32},{96,64},{1,97},{33,1},{65,33},{97,65},{2,98}... | collective-permute-start | bytes 540680 | tf_op jit(solution)/shard_map/ppermute | solution.py:349
  143.2 9.3 %collective-permute-start.2 = (f32[44,8,128]{2,1,0:T(8,128)}, f32[44,8,128]{2,1,0:T(8,128)}, u32[]{:S(2)}, u32[]{:S(2)}) collective-permute-start(f32[44,8,128]{2,1,0:T(8,128)} %get-tuple-element.35), channel_id=1, source_target_pairs={{0,64},{32,96},{64,0},{96,32},{1,65},{33,97},{65,1},{97,33},{2,66}... | collective-permute-start | bytes 540680 | tf_op jit(solution)/shard_map/ppermute | solution.py:349
  143.8 11.4 %collective-permute-start.1 = (f32[44,8,128]{2,1,0:T(8,128)}, f32[44,8,128]{2,1,0:T(8,128)}, u32[]{:S(2)}, u32[]{:S(2)}) collective-permute-start(f32[44,8,128]{2,1,0:T(8,128)} %get-tuple-element.33), channel_id=1, source_target_pairs={{0,32},{32,64},{64,96},{96,0},{1,33},{33,65},{65,97},{97,1},{2,34}... | collective-permute-start | bytes 540680 | tf_op jit(solution)/shard_map/ppermute | solution.py:349
  151.5 1.0 copy-start.1
  156.4 6.7 %collective-permute-start.6 = (f32[11,8,128]{2,1,0:T(8,128)S(1)}, f32[11,8,128]{2,1,0:T(8,128)S(1)}, u32[]{:S(2)}, u32[]{:S(2)}) collective-permute-start(f32[11,8,128]{2,1,0:T(8,128)S(1)} %get-tuple-element.39), channel_id=1, source_target_pairs={{0,3},{1,0},{2,1},{3,2},{4,7},{5,4},{6,5},{7,6},{8,11},{9,8},{10,9... | collective-permute-start | bytes 135176 | tf_op jit(solution)/shard_map/ppermute | solution.py:349
  159.2 5.6 %collective-permute-start.5 = (f32[11,8,128]{2,1,0:T(8,128)S(1)}, f32[11,8,128]{2,1,0:T(8,128)S(1)}, u32[]{:S(2)}, u32[]{:S(2)}) collective-permute-start(f32[11,8,128]{2,1,0:T(8,128)S(1)} %get-tuple-element.40), channel_id=1, source_target_pairs={{0,2},{1,3},{2,0},{3,1},{4,6},{5,7},{6,4},{7,5},{8,10},{9,11},{10,... | collective-permute-start | bytes 135176 | tf_op jit(solution)/shard_map/ppermute | solution.py:349
  160.1 5.3 %collective-permute-start.4 = (f32[11,8,128]{2,1,0:T(8,128)S(1)}, f32[11,8,128]{2,1,0:T(8,128)S(1)}, u32[]{:S(2)}, u32[]{:S(2)}) collective-permute-start(f32[11,8,128]{2,1,0:T(8,128)S(1)} %get-tuple-element.38), channel_id=1, source_target_pairs={{0,1},{1,2},{2,3},{3,0},{4,5},{5,6},{6,7},{7,4},{8,9},{9,10},{10,1... | collective-permute-start | bytes 135176 | tf_op jit(solution)/shard_map/ppermute | solution.py:349
  165.3 8.5 %collective-permute-start.7 = (f32[11,8,128]{2,1,0:T(8,128)S(1)}, f32[11,8,128]{2,1,0:T(8,128)S(1)}, u32[]{:S(2)}, u32[]{:S(2)}) collective-permute-start(f32[11,8,128]{2,1,0:T(8,128)S(1)} %add_add_fusion.1), channel_id=1, source_target_pairs={{0,128},{128,0},{1,129},{129,1},{2,130},{130,2},{3,131},{131,3},{4... | collective-permute-start | bytes 135176 | tf_op jit(solution)/shard_map/ppermute | solution.py:378
  173.8 6.7 %collective-permute-start.10 = (f32[11,8,128]{2,1,0:T(8,128)S(1)}, f32[11,8,128]{2,1,0:T(8,128)S(1)}, u32[]{:S(2)}, u32[]{:S(2)}) collective-permute-start(f32[11,8,128]{2,1,0:T(8,128)S(1)} %add_multiply_fusion), channel_id=1, source_target_pairs={{0,12},{4,0},{8,4},{12,8},{1,13},{5,1},{9,5},{13,9},{2,14},{6,2},{... | collective-permute-start | bytes 135176 | tf_op jit(solution)/shard_map/ppermute | solution.py:349
  178.4 4.9 %collective-permute-start.9 = (f32[11,8,128]{2,1,0:T(8,128)S(1)}, f32[11,8,128]{2,1,0:T(8,128)S(1)}, u32[]{:S(2)}, u32[]{:S(2)}) collective-permute-start(f32[11,8,128]{2,1,0:T(8,128)S(1)} %add_multiply_fusion), channel_id=1, source_target_pairs={{0,8},{4,12},{8,0},{12,4},{1,9},{5,13},{9,1},{13,5},{2,10},{6,14},... | collective-permute-start | bytes 135176 | tf_op jit(solution)/shard_map/ppermute | solution.py:349
  179.9 4.0 %collective-permute-start.8 = (f32[11,8,128]{2,1,0:T(8,128)S(1)}, f32[11,8,128]{2,1,0:T(8,128)S(1)}, u32[]{:S(2)}, u32[]{:S(2)}) collective-permute-start(f32[11,8,128]{2,1,0:T(8,128)S(1)} %add_multiply_fusion), channel_id=1, source_target_pairs={{0,4},{4,8},{8,12},{12,0},{1,5},{5,9},{9,13},{13,1},{2,6},{6,10},{... | collective-permute-start | bytes 135176 | tf_op jit(solution)/shard_map/ppermute | solution.py:349
  184.0 40.9 %all-to-all-start.2 = ((bf16[16,2,6,16,256]{4,3,2,1,0:T(8,128)(2,1)}), bf16[16,2,6,16,256]{4,3,2,1,0:T(8,128)(2,1)}, u32[]{:S(2)}, u32[]{:S(2)}) async-start(bf16[16,2,6,16,256]{4,3,2,1,0:T(8,128)(2,1)} %get-tuple-element.23), calls=%async_computation.2 | async-start | bytes 3145728 | tf_op jit(solution)/shard_map/all_to_all | solution.py:436
  190.1 8.0 %collective-permute-start.11 = (f32[11,8,128]{2,1,0:T(8,128)S(1)}, f32[11,8,128]{2,1,0:T(8,128)S(1)}, u32[]{:S(2)}, u32[]{:S(2)}) collective-permute-start(f32[11,8,128]{2,1,0:T(8,128)S(1)} %add_bitcast_fusion), channel_id=1, source_target_pairs={{0,1},{1,2},{2,3},{3,0},{4,5},{5,6},{6,7},{7,4},{8,9},{9,10},{10,1... | collective-permute-start | bytes 135176 | tf_op jit(solution)/shard_map/ppermute | solution.py:349
  191.6 7.3 %collective-permute-start.12 = (f32[11,8,128]{2,1,0:T(8,128)S(1)}, f32[11,8,128]{2,1,0:T(8,128)S(1)}, u32[]{:S(2)}, u32[]{:S(2)}) collective-permute-start(f32[11,8,128]{2,1,0:T(8,128)S(1)} %add_bitcast_fusion), channel_id=1, source_target_pairs={{0,2},{1,3},{2,0},{3,1},{4,6},{5,7},{6,4},{7,5},{8,10},{9,11},{10,... | collective-permute-start | bytes 135176 | tf_op jit(solution)/shard_map/ppermute | solution.py:349
  194.2 4.9 %collective-permute-start.13 = (f32[11,8,128]{2,1,0:T(8,128)S(1)}, f32[11,8,128]{2,1,0:T(8,128)S(1)}, u32[]{:S(2)}, u32[]{:S(2)}) collective-permute-start(f32[11,8,128]{2,1,0:T(8,128)S(1)} %add_bitcast_fusion), channel_id=1, source_target_pairs={{0,3},{1,0},{2,1},{3,2},{4,7},{5,4},{6,5},{7,6},{8,11},{9,8},{10,9... | collective-permute-start | bytes 135176 | tf_op jit(solution)/shard_map/ppermute | solution.py:349
  199.2 9.5 %collective-permute-start.14 = (f32[44,8,128]{2,1,0:T(8,128)S(1)}, f32[44,8,128]{2,1,0:T(8,128)S(1)}, u32[]{:S(2)}, u32[]{:S(2)}) collective-permute-start(f32[44,8,128]{2,1,0:T(8,128)S(1)} %constant_dynamic-update-slice_fusion.3), channel_id=1, source_target_pairs={{0,32},{32,64},{64,96},{96,0},{1,33},{33,65},{65,97},{97,1},{2,34}... | collective-permute-start | bytes 540680 | tf_op jit(solution)/shard_map/ppermute | solution.py:349
  199.2 9.5 %collective-permute-start.15 = (f32[44,8,128]{2,1,0:T(8,128)S(1)}, f32[44,8,128]{2,1,0:T(8,128)S(1)}, u32[]{:S(2)}, u32[]{:S(2)}) collective-permute-start(f32[44,8,128]{2,1,0:T(8,128)S(1)} %constant_dynamic-update-slice_fusion.3), channel_id=1, source_target_pairs={{0,64},{32,96},{64,0},{96,32},{1,65},{33,97},{65,1},{97,33},{2,66}... | collective-permute-start | bytes 540680 | tf_op jit(solution)/shard_map/ppermute | solution.py:349
  201.8 6.9 %collective-permute-start.16 = (f32[44,8,128]{2,1,0:T(8,128)S(1)}, f32[44,8,128]{2,1,0:T(8,128)S(1)}, u32[]{:S(2)}, u32[]{:S(2)}) collective-permute-start(f32[44,8,128]{2,1,0:T(8,128)S(1)} %constant_dynamic-update-slice_fusion.3), channel_id=1, source_target_pairs={{0,96},{32,0},{64,32},{96,64},{1,97},{33,1},{65,33},{97,65},{2,98}... | collective-permute-start | bytes 540680 | tf_op jit(solution)/shard_map/ppermute | solution.py:349
  208.7 2.3 %collective-permute-start.17 = (f32[176,8,128]{2,1,0:T(8,128)S(1)}, f32[176,8,128]{2,1,0:T(8,128)S(1)}, u32[]{:S(2)}, u32[]{:S(2)}) collective-permute-start(f32[176,8,128]{2,1,0:T(8,128)S(1)} %constant_dynamic-update-slice_fusion.4.own_ref), channel_id=1, source_target_pairs={{0,16},{16,0},{1,17},{17,1},{2,18},{18,2},{3,19},{19,3},{4,20},{20... | collective-permute-start | bytes 2162696 | tf_op jit(solution)/shard_map/ppermute | solution.py:378

commit v2 on v1

--- a/solution.py
+++ b/solution.py
@@ -59,8 +59,8 @@
     for n in range(units):
         for which in range(2):
             arrival(n, which).wait()
-            turned = jnp.swapaxes(held[n, which], 0, 1)
-            made[n, :, which] = turned.reshape(MEMBERS, PAIRS, 16, C)
+            turned = jnp.swapaxes(held[n, which].astype(F32), 0, 1)
+            made[n, :, which] = turned.reshape(MEMBERS, PAIRS, 16, C).astype(BF16)
         departure(n).start()
     for n in range(units):
         departure(n).wait()
@@ -100,8 +100,8 @@
     for n in range(units):
         arrival(n).wait()
         for which in range(2):
-            turned = held[n, :, which].reshape(COUNT, OWN_ROWS, C)
-            made[n, which] = jnp.swapaxes(turned, 0, 1)
+            turned = held[n, :, which].astype(F32).reshape(COUNT, OWN_ROWS, C)
+            made[n, which] = jnp.swapaxes(turned, 0, 1).astype(BF16)
             departure(n, which).start()
     for n in range(units):
         for which in range(2):

time: 230 us -> 232 us (level)
  transfers between devices with their start and end apart: 22 -> 22, of which waited for: 19 -> 19; matrix products, arithmetic and copies ran while one was open for 4% -> 4% of each run, Pallas kernels for 21% -> 22%
where the time goes in v2:
time: 232 us; the launch traced here: 228 us
  waiting for transfers between devices  105 us (45%)
  starting transfers between devices  57.8 us (25%)
  Pallas kernels  55.1 us (24%)
  other arithmetic  5.63 us (2%)
  local copies, waits for them, and re-layouts  3.19 us (1%)
    all_to_all x4, waiting for transfers between devices, exchange(): return lax.all_to_all(value, DAP, 0, 0, tiled=True)  70.2 us
    pallas_call x2, Pallas kernels, columns(): pl.pallas_call(functools.partial(pair_kernel, steps, sums is not None, la...  43.5 us
    all_to_all x4, starting transfers between devices, exchange(): return lax.all_to_all(value, DAP, 0, 0, tiled=True)  27.2 us
    ppermute x15, waiting for transfers between devices, shift(): lax.ppermute(value, axes, [(k, (k + step) % size) for k in range(size)])  26.4 us
    ppermute x15, starting transfers between devices, shift(): lax.ppermute(value, axes, [(k, (k + step) % size) for k in range(size)])  26 us
    ppermute x3, waiting for transfers between devices, swap(): return lax.ppermute(value, axis, [(0, 1), (1, 0)])  8.53 us
    pallas_call x2, Pallas kernels, pack(): pl.pallas_call(functools.partial(pack_kernel, first, units), in_specs=[an...  5.69 us
    pallas_call x2, Pallas kernels, unpack(): pl.pallas_call(functools.partial(unpack_kernel, first, units), in_specs=[...  4.73 us
  transfers between devices with their start and end apart: 22, of which 19 were waited for; matrix products, arithmetic and copies ran while one was open for 4% of the time, Pallas kernels for 22%

profile of v2, /device:TPU:32, one launch (start us, length us, event | category | flops | bytes accessed | tf_op | source)
XLA Modules:
  0.0 228.0 jit_solution(18090016418326289426)
XLA Ops:
  0.6 3.1 %shard_map.147 = bf16[16,2,10,16,256]{4,3,2,1,0:T(8,128)(2,1)} custom-call(bf16[2,8,256,256]{3,2,1,0:T(8,128)(2,1)} %x_ref.3, bf16[2,8,256,256]{3,2,1,0:T(8,128)(2,1)} %cot_ref.3), custom_call_target="tpu_custom_call" | custom-call | bytes 5242880 | tf_op jit(solution)/shard_map/pallas_call | solution.py:71
  3.7 8.5 %all-to-all-start.1 = ((bf16[16,2,10,16,256]{4,3,2,1,0:T(8,128)(2,1)}), bf16[16,2,10,16,256]{4,3,2,1,0:T(8,128)(2,1)S(1)}, u32[]{:S(2)}, u32[]{:S(2)}) async-start(bf16[16,2,10,16,256]{4,3,2,1,0:T(8,128)(2,1)} %shard_map.147), calls=%async_computation.1 | async-start | bytes 5242880 | tf_op jit(solution)/shard_map/all_to_all | solution.py:436
  12.3 2.6 %shard_map.146 = bf16[16,2,6,16,256]{4,3,2,1,0:T(8,128)(2,1)} custom-call(bf16[2,8,256,256]{3,2,1,0:T(8,128)(2,1)} %x_ref.3, bf16[2,8,256,256]{3,2,1,0:T(8,128)(2,1)} %cot_ref.3), custom_call_target="tpu_custom_call" | custom-call | bytes 3145728 | tf_op jit(solution)/shard_map/pallas_call | solution.py:71
  16.0 1.8 fusion
  19.6 50.6 %all-to-all-done.1.refs_1_.refs_2_ = bf16[16,2,10,16,256]{4,3,2,1,0:T(8,128)(2,1)S(1)} async-done(((bf16[16,2,10,16,256]{4,3,2,1,0:T(8,128)(2,1)}), bf16[16,2,10,16,256]{4,3,2,1,0:T(8,128)(2,1)S(1)}, u32[]{:S(2)}, u32[]{:S(2)}) %all-to-all-start.1) | async-done | bytes 2621472 | tf_op jit(solution)/shard_map/all_to_all | solution.py:436
  70.2 7.0 %all-to-all-start = ((bf16[16,2,6,16,256]{4,3,2,1,0:T(8,128)(2,1)}), bf16[16,2,6,16,256]{4,3,2,1,0:T(8,128)(2,1)}, u32[]{:S(2)}, u32[]{:S(2)}) async-start(bf16[16,2,6,16,256]{4,3,2,1,0:T(8,128)(2,1)} %shard_map.146), calls=%async_computation | async-start | bytes 3145728 | tf_op jit(solution)/shard_map/all_to_all | solution.py:436
  78.0 25.9 %shard_map.148 = (bf16[16,2,10,16,256]{4,3,2,1,0:T(8,128)(2,1)}, f32[2,176,8,128]{3,2,1,0:T(8,128)}) custom-call(s32[1]{0:T(128)} %bitcast.refs_0_.core_ref, bf16[16,2,10,16,256]{4,3,2,1,0:T(8,128)(2,1)} %copy-done, bf16[16,2,10,16,256]{4,3,2,1,0:T(8,128)(2,1)} %copy-done, bf16[256,1024]{1,0:T(8,128)(2,1)} %copy.23.refs_3_, ...), custom_call_target="tpu_custom_call" | custom-call | flops 40000000000 | bytes 8388608 | tf_op jit(solution)/shard_map/pallas_call | solution.py:332
  103.9 9.2 %all-to-all-done.refs_1_.refs_2_ = bf16[16,2,6,16,256]{4,3,2,1,0:T(8,128)(2,1)} async-done(((bf16[16,2,6,16,256]{4,3,2,1,0:T(8,128)(2,1)}), bf16[16,2,6,16,256]{4,3,2,1,0:T(8,128)(2,1)}, u32[]{:S(2)}, u32[]{:S(2)}) %all-to-all-start) | async-done | bytes 1572896 | tf_op jit(solution)/shard_map/all_to_all | solution.py:436
  113.1 5.6 %all-to-all-start.3 = ((bf16[16,2,10,16,256]{4,3,2,1,0:T(8,128)(2,1)}), bf16[16,2,10,16,256]{4,3,2,1,0:T(8,128)(2,1)S(1)}, u32[]{:S(2)}, u32[]{:S(2)}) async-start(bf16[16,2,10,16,256]{4,3,2,1,0:T(8,128)(2,1)} %get-tuple-element.24), calls=%async_computation.3 | async-start | bytes 5242880 | tf_op jit(solution)/shard_map/all_to_all | solution.py:436
  118.7 17.6 %shard_map.149 = (bf16[16,2,6,16,256]{4,3,2,1,0:T(8,128)(2,1)}, f32[176,8,128]{2,1,0:T(8,128)}, f32[176,8,128]{2,1,0:T(8,128)}) custom-call(s32[1]{0:T(128)} %bitcast.refs_0_.core_ref, bf16[16,2,6,16,256]{4,3,2,1,0:T(8,128)(2,1)} %all-to-all-done.refs_1_.refs_2_, bf16[16,2,6,16,256]{4,3,2,1,0:T(8,128)(2,1)} %all-to-all-done.refs_1_.refs_2_, ...), custom_call_target="tpu_custom_call" | custom-call | flops 24000000000 | bytes 8388608 | tf_op jit(solution)/shard_map/pallas_call | solution.py:332
  136.3 2.4 %collective-permute-done = f32[176,8,128]{2,1,0:T(8,128)S(1)} collective-permute-done((f32[176,8,128]{2,1,0:T(8,128)}, f32[176,8,128]{2,1,0:T(8,128)S(1)}, u32[]{:S(2)}, u32[]{:S(2)}) %collective-permute-start) | collective-permute-done | bytes 720928 | tf_op jit(solution)/shard_map/ppermute | solution.py:378
  138.7 1.9 dynamic-slice_add_fusion.2
  140.6 3.0 %collective-permute-start.3 = (f32[44,8,128]{2,1,0:T(8,128)}, f32[44,8,128]{2,1,0:T(8,128)S(1)}, u32[]{:S(2)}, u32[]{:S(2)}) collective-permute-start(f32[44,8,128]{2,1,0:T(8,128)} %get-tuple-element.34), channel_id=1, source_target_pairs={{0,96},{32,0},{64,32},{96,64},{1,97},{33,1},{65,33},{97,65},{2,98}... | collective-permute-start | bytes 540680 | tf_op jit(solution)/shard_map/ppermute | solution.py:349
  145.2 6.7 %collective-permute-done.3 = f32[44,8,128]{2,1,0:T(8,128)S(1)} collective-permute-done((f32[44,8,128]{2,1,0:T(8,128)}, f32[44,8,128]{2,1,0:T(8,128)S(1)}, u32[]{:S(2)}, u32[]{:S(2)}) %collective-permute-start.3) | collective-permute-done | bytes 180256 | tf_op jit(solution)/shard_map/ppermute | solution.py:349
  152.9 2.7 %collective-permute-done.1 = f32[44,8,128]{2,1,0:T(8,128)} collective-permute-done((f32[44,8,128]{2,1,0:T(8,128)}, f32[44,8,128]{2,1,0:T(8,128)}, u32[]{:S(2)}, u32[]{:S(2)}) %collective-permute-start.1) | collective-permute-done | bytes 180256 | tf_op jit(solution)/shard_map/ppermute | solution.py:349
  156.9 2.7 %collective-permute-start.6 = (f32[11,8,128]{2,1,0:T(8,128)S(1)}, f32[11,8,128]{2,1,0:T(8,128)S(1)}, u32[]{:S(2)}, u32[]{:S(2)}) collective-permute-start(f32[11,8,128]{2,1,0:T(8,128)S(1)} %get-tuple-element.39), channel_id=1, source_target_pairs={{0,3},{1,0},{2,1},{3,2},{4,7},{5,4},{6,5},{7,6},{8,11},{9,8},{10,9... | collective-permute-start | bytes 135176 | tf_op jit(solution)/shard_map/ppermute | solution.py:349
  161.3 2.2 collective-permute-done.6
  163.5 1.6 collective-permute-done.5
  165.8 4.5 %collective-permute-start.7 = (f32[11,8,128]{2,1,0:T(8,128)S(1)}, f32[11,8,128]{2,1,0:T(8,128)S(1)}, u32[]{:S(2)}, u32[]{:S(2)}) collective-permute-start(f32[11,8,128]{2,1,0:T(8,128)S(1)} %add_add_fusion.1), channel_id=1, source_target_pairs={{0,128},{128,0},{1,129},{129,1},{2,130},{130,2},{3,131},{131,3},{4... | collective-permute-start | bytes 135176 | tf_op jit(solution)/shard_map/ppermute | solution.py:378
  170.3 4.0 %collective-permute-done.7 = f32[11,8,128]{2,1,0:T(8,128)S(1)} collective-permute-done((f32[11,8,128]{2,1,0:T(8,128)S(1)}, f32[11,8,128]{2,1,0:T(8,128)S(1)}, u32[]{:S(2)}, u32[]{:S(2)}) %collective-permute-start.7) | collective-permute-done | bytes 45088 | tf_op jit(solution)/shard_map/ppermute | solution.py:378
  174.2 4.5 %collective-permute-start.10 = (f32[11,8,128]{2,1,0:T(8,128)S(1)}, f32[11,8,128]{2,1,0:T(8,128)S(1)}, u32[]{:S(2)}, u32[]{:S(2)}) collective-permute-start(f32[11,8,128]{2,1,0:T(8,128)S(1)} %add_multiply_fusion), channel_id=1, source_target_pairs={{0,12},{4,0},{8,4},{12,8},{1,13},{5,1},{9,5},{13,9},{2,14},{6,2},{... | collective-permute-start | bytes 135176 | tf_op jit(solution)/shard_map/ppermute | solution.py:349
  180.9 2.8 %collective-permute-done.9 = f32[11,8,128]{2,1,0:T(8,128)S(1)} collective-permute-done((f32[11,8,128]{2,1,0:T(8,128)S(1)}, f32[11,8,128]{2,1,0:T(8,128)S(1)}, u32[]{:S(2)}, u32[]{:S(2)}) %collective-permute-start.9) | collective-permute-done | bytes 45088 | tf_op jit(solution)/shard_map/ppermute | solution.py:349
  184.5 6.1 %all-to-all-start.2 = ((bf16[16,2,6,16,256]{4,3,2,1,0:T(8,128)(2,1)}), bf16[16,2,6,16,256]{4,3,2,1,0:T(8,128)(2,1)}, u32[]{:S(2)}, u32[]{:S(2)}) async-start(bf16[16,2,6,16,256]{4,3,2,1,0:T(8,128)(2,1)} %get-tuple-element.23), calls=%async_computation.2 | async-start | bytes 3145728 | tf_op jit(solution)/shard_map/all_to_all | solution.py:436
  192.0 2.7 %collective-permute-start.12 = (f32[11,8,128]{2,1,0:T(8,128)S(1)}, f32[11,8,128]{2,1,0:T(8,128)S(1)}, u32[]{:S(2)}, u32[]{:S(2)}) collective-permute-start(f32[11,8,128]{2,1,0:T(8,128)S(1)} %add_bitcast_fusion), channel_id=1, source_target_pairs={{0,2},{1,3},{2,0},{3,1},{4,6},{5,7},{6,4},{7,5},{8,10},{9,11},{10,... | collective-permute-start | bytes 135176 | tf_op jit(solution)/shard_map/ppermute | solution.py:349
  196.2 2.3 %collective-permute-done.11 = f32[11,8,128]{2,1,0:T(8,128)S(1)} collective-permute-done((f32[11,8,128]{2,1,0:T(8,128)S(1)}, f32[11,8,128]{2,1,0:T(8,128)S(1)}, u32[]{:S(2)}, u32[]{:S(2)}) %collective-permute-start.11) | collective-permute-done | bytes 45088 | tf_op jit(solution)/shard_map/ppermute | solution.py:349
  199.6 2.7 %collective-permute-start.15 = (f32[44,8,128]{2,1,0:T(8,128)S(1)}, f32[44,8,128]{2,1,0:T(8,128)S(1)}, u32[]{:S(2)}, u32[]{:S(2)}) collective-permute-start(f32[44,8,128]{2,1,0:T(8,128)S(1)} %constant_dynamic-update-slice_fusion.3), channel_id=1, source_target_pairs={{0,64},{32,96},{64,0},{96,32},{1,65},{33,97},{65,1},{97,33},{2,66}... | collective-permute-start | bytes 540680 | tf_op jit(solution)/shard_map/ppermute | solution.py:349
  202.3 2.5 %collective-permute-start.16 = (f32[44,8,128]{2,1,0:T(8,128)S(1)}, f32[44,8,128]{2,1,0:T(8,128)S(1)}, u32[]{:S(2)}, u32[]{:S(2)}) collective-permute-start(f32[44,8,128]{2,1,0:T(8,128)S(1)} %constant_dynamic-update-slice_fusion.3), channel_id=1, source_target_pairs={{0,96},{32,0},{64,32},{96,64},{1,97},{33,1},{65,33},{97,65},{2,98}... | collective-permute-start | bytes 540680 | tf_op jit(solution)/shard_map/ppermute | solution.py:349
  204.9 4.2 %collective-permute-done.14 = f32[44,8,128]{2,1,0:T(8,128)S(1)} collective-permute-done((f32[44,8,128]{2,1,0:T(8,128)S(1)}, f32[44,8,128]{2,1,0:T(8,128)S(1)}, u32[]{:S(2)}, u32[]{:S(2)}) %collective-permute-start.14) | collective-permute-done | bytes 180256 | tf_op jit(solution)/shard_map/ppermute | solution.py:349
  209.3 2.2 collective-permute-done.17.other_ref
  212.6 2.2 shard_map.150
  214.8 10.5 %all-to-all-done.2.refs_0_ = bf16[16,2,6,16,256]{4,3,2,1,0:T(8,128)(2,1)} async-done(((bf16[16,2,6,16,256]{4,3,2,1,0:T(8,128)(2,1)}), bf16[16,2,6,16,256]{4,3,2,1,0:T(8,128)(2,1)}, u32[]{:S(2)}, u32[]{:S(2)}) %all-to-all-start.2) | async-done | bytes 1572896 | tf_op jit(solution)/shard_map/all_to_all | solution.py:436
  225.3 2.5 %shard_map.151 = (bf16[2,8,256,256]{3,2,1,0:T(8,128)(2,1)}, bf16[2,8,256,256]{3,2,1,0:T(8,128)(2,1)}) custom-call(bf16[16,2,6,16,256]{4,3,2,1,0:T(8,128)(2,1)} %all-to-all-done.2.refs_0_, bf16[2,8,256,256]{3,2,1,0:T(8,128)(2,1)} %get-tuple-element.25.refs_1_, ...), custom_call_target="tpu_custom_call", output_to_operand_aliasing={{0}: (1, {}), {1}: (2, {})} | custom-call | bytes 3145728 | tf_op jit(solution)/shard_map/pallas_call | solution.py:115
  (66 shorter events, 18.2 us)
Async XLA Ops:
  3.7 66.5 %all-to-all-start.1 = ((bf16[16,2,10,16,256]{4,3,2,1,0:T(8,128)(2,1)}), bf16[16,2,10,16,256]{4,3,2,1,0:T(8,128)(2,1)S(1)}, u32[]{:S(2)}, u32[]{:S(2)}) async-start(bf16[16,2,10,16,256]{4,3,2,1,0:T(8,128)(2,1)} %shard_map.147), calls=%async_computation.1 | async-start | bytes 5242880 | tf_op jit(solution)/shard_map/all_to_all | solution.py:436
  12.2 2.7 %copy-start.2 = (bf16[256,256]{1,0:T(8,128)(2,1)S(1)}, bf16[256,256]{1,0:T(8,128)(2,1)}, u32[]{:S(2)}) copy-start(bf16[256,256]{1,0:T(8,128)(2,1)} %param.16) | copy-start | bytes 393220
  12.2 2.8 %copy-start.3 = (bf16[256,256]{1,0:T(8,128)(2,1)S(1)}, bf16[256,256]{1,0:T(8,128)(2,1)}, u32[]{:S(2)}) copy-start(bf16[256,256]{1,0:T(8,128)(2,1)} %param.15) | copy-start | bytes 393220
  12.2 2.9 %copy-start.4 = (bf16[256,256]{1,0:T(8,128)(2,1)S(1)}, bf16[256,256]{1,0:T(8,128)(2,1)}, u32[]{:S(2)}) copy-start(bf16[256,256]{1,0:T(8,128)(2,1)} %param.14) | copy-start | bytes 393220
  12.3 3.0 %copy-start.5 = (bf16[256,256]{1,0:T(8,128)(2,1)S(1)}, bf16[256,256]{1,0:T(8,128)(2,1)}, u32[]{:S(2)}) copy-start(bf16[256,256]{1,0:T(8,128)(2,1)} %param.13) | copy-start | bytes 393220
  14.9 4.1 %copy-start.7 = (f32[256]{0:T(256)S(1)}, f32[256]{0:T(256)}, u32[]{:S(2)}) copy-start(f32[256]{0:T(256)} %param.21) | copy-start | bytes 3076
  14.9 4.1 %copy-start.8 = (f32[256]{0:T(256)S(1)}, f32[256]{0:T(256)}, u32[]{:S(2)}) copy-start(f32[256]{0:T(256)} %param.20) | copy-start | bytes 3076
  14.9 4.0 %copy-start.9 = (f32[256]{0:T(256)S(1)}, f32[256]{0:T(256)}, u32[]{:S(2)}) copy-start(f32[256]{0:T(256)} %param.19) | copy-start | bytes 3076
  17.8 59.4 %copy-start.6 = (f32[256]{0:T(256)S(1)}, f32[256]{0:T(256)}, u32[]{:S(2)}) copy-start(f32[256]{0:T(256)} %param.17) | copy-start | bytes 3076
  70.2 7.8 %copy-start = (bf16[16,2,10,16,256]{4,3,2,1,0:T(8,128)(2,1)}, bf16[16,2,10,16,256]{4,3,2,1,0:T(8,128)(2,1)S(1)}, u32[]{:S(2)}) copy-start(bf16[16,2,10,16,256]{4,3,2,1,0:T(8,128)(2,1)S(1)} %all-to-all-done.1.refs_1_.refs_2_) | copy-start | bytes 7864324
  70.2 42.9 %all-to-all-start = ((bf16[16,2,6,16,256]{4,3,2,1,0:T(8,128)(2,1)}), bf16[16,2,6,16,256]{4,3,2,1,0:T(8,128)(2,1)}, u32[]{:S(2)}, u32[]{:S(2)}) async-start(bf16[16,2,6,16,256]{4,3,2,1,0:T(8,128)(2,1)} %shard_map.146), calls=%async_computation | async-start | bytes 3145728 | tf_op jit(solution)/shard_map/all_to_all | solution.py:436
  113.1 71.4 %all-to-all-start.3 = ((bf16[16,2,10,16,256]{4,3,2,1,0:T(8,128)(2,1)}), bf16[16,2,10,16,256]{4,3,2,1,0:T(8,128)(2,1)S(1)}, u32[]{:S(2)}, u32[]{:S(2)}) async-start(bf16[16,2,10,16,256]{4,3,2,1,0:T(8,128)(2,1)} %get-tuple-element.24), calls=%async_computation.3 | async-start | bytes 5242880 | tf_op jit(solution)/shard_map/all_to_all | solution.py:436
  136.3 2.4 %collective-permute-start = (f32[176,8,128]{2,1,0:T(8,128)}, f32[176,8,128]{2,1,0:T(8,128)S(1)}, u32[]{:S(2)}, u32[]{:S(2)}) collective-permute-start(f32[176,8,128]{2,1,0:T(8,128)} %get-tuple-element.21), channel_id=1, source_target_pairs={{0,16},{16,0},{1,17},{17,1},{2,18},{18,2},{3,19},{19,3},{4,20},{20... | collective-permute-start | bytes 2162696 | tf_op jit(solution)/shard_map/ppermute | solution.py:378
  140.6 11.3 %collective-permute-start.3 = (f32[44,8,128]{2,1,0:T(8,128)}, f32[44,8,128]{2,1,0:T(8,128)S(1)}, u32[]{:S(2)}, u32[]{:S(2)}) collective-permute-start(f32[44,8,128]{2,1,0:T(8,128)} %get-tuple-element.34), channel_id=1, source_target_pairs={{0,96},{32,0},{64,32},{96,64},{1,97},{33,1},{65,33},{97,65},{2,98}... | collective-permute-start | bytes 540680 | tf_op jit(solution)/shard_map/ppermute | solution.py:349
  143.6 9.3 %collective-permute-start.2 = (f32[44,8,128]{2,1,0:T(8,128)}, f32[44,8,128]{2,1,0:T(8,128)}, u32[]{:S(2)}, u32[]{:S(2)}) collective-permute-start(f32[44,8,128]{2,1,0:T(8,128)} %get-tuple-element.35), channel_id=1, source_target_pairs={{0,64},{32,96},{64,0},{96,32},{1,65},{33,97},{65,1},{97,33},{2,66}... | collective-permute-start | bytes 540680 | tf_op jit(solution)/shard_map/ppermute | solution.py:349
  144.2 11.4 %collective-permute-start.1 = (f32[44,8,128]{2,1,0:T(8,128)}, f32[44,8,128]{2,1,0:T(8,128)}, u32[]{:S(2)}, u32[]{:S(2)}) collective-permute-start(f32[44,8,128]{2,1,0:T(8,128)} %get-tuple-element.33), channel_id=1, source_target_pairs={{0,32},{32,64},{64,96},{96,0},{1,33},{33,65},{65,97},{97,1},{2,34}... | collective-permute-start | bytes 540680 | tf_op jit(solution)/shard_map/ppermute | solution.py:349
  151.9 1.0 copy-start.1
  156.9 6.6 %collective-permute-start.6 = (f32[11,8,128]{2,1,0:T(8,128)S(1)}, f32[11,8,128]{2,1,0:T(8,128)S(1)}, u32[]{:S(2)}, u32[]{:S(2)}) collective-permute-start(f32[11,8,128]{2,1,0:T(8,128)S(1)} %get-tuple-element.39), channel_id=1, source_target_pairs={{0,3},{1,0},{2,1},{3,2},{4,7},{5,4},{6,5},{7,6},{8,11},{9,8},{10,9... | collective-permute-start | bytes 135176 | tf_op jit(solution)/shard_map/ppermute | solution.py:349
  159.6 5.6 %collective-permute-start.5 = (f32[11,8,128]{2,1,0:T(8,128)S(1)}, f32[11,8,128]{2,1,0:T(8,128)S(1)}, u32[]{:S(2)}, u32[]{:S(2)}) collective-permute-start(f32[11,8,128]{2,1,0:T(8,128)S(1)} %get-tuple-element.40), channel_id=1, source_target_pairs={{0,2},{1,3},{2,0},{3,1},{4,6},{5,7},{6,4},{7,5},{8,10},{9,11},{10,... | collective-permute-start | bytes 135176 | tf_op jit(solution)/shard_map/ppermute | solution.py:349
  160.5 5.3 %collective-permute-start.4 = (f32[11,8,128]{2,1,0:T(8,128)S(1)}, f32[11,8,128]{2,1,0:T(8,128)S(1)}, u32[]{:S(2)}, u32[]{:S(2)}) collective-permute-start(f32[11,8,128]{2,1,0:T(8,128)S(1)} %get-tuple-element.38), channel_id=1, source_target_pairs={{0,1},{1,2},{2,3},{3,0},{4,5},{5,6},{6,7},{7,4},{8,9},{9,10},{10,1... | collective-permute-start | bytes 135176 | tf_op jit(solution)/shard_map/ppermute | solution.py:349
  165.8 8.5 %collective-permute-start.7 = (f32[11,8,128]{2,1,0:T(8,128)S(1)}, f32[11,8,128]{2,1,0:T(8,128)S(1)}, u32[]{:S(2)}, u32[]{:S(2)}) collective-permute-start(f32[11,8,128]{2,1,0:T(8,128)S(1)} %add_add_fusion.1), channel_id=1, source_target_pairs={{0,128},{128,0},{1,129},{129,1},{2,130},{130,2},{3,131},{131,3},{4... | collective-permute-start | bytes 135176 | tf_op jit(solution)/shard_map/ppermute | solution.py:378
  174.2 6.7 %collective-permute-start.10 = (f32[11,8,128]{2,1,0:T(8,128)S(1)}, f32[11,8,128]{2,1,0:T(8,128)S(1)}, u32[]{:S(2)}, u32[]{:S(2)}) collective-permute-start(f32[11,8,128]{2,1,0:T(8,128)S(1)} %add_multiply_fusion), channel_id=1, source_target_pairs={{0,12},{4,0},{8,4},{12,8},{1,13},{5,1},{9,5},{13,9},{2,14},{6,2},{... | collective-permute-start | bytes 135176 | tf_op jit(solution)/shard_map/ppermute | solution.py:349
  178.8 4.9 %collective-permute-start.9 = (f32[11,8,128]{2,1,0:T(8,128)S(1)}, f32[11,8,128]{2,1,0:T(8,128)S(1)}, u32[]{:S(2)}, u32[]{:S(2)}) collective-permute-start(f32[11,8,128]{2,1,0:T(8,128)S(1)} %add_multiply_fusion), channel_id=1, source_target_pairs={{0,8},{4,12},{8,0},{12,4},{1,9},{5,13},{9,1},{13,5},{2,10},{6,14},... | collective-permute-start | bytes 135176 | tf_op jit(solution)/shard_map/ppermute | solution.py:349
  180.4 4.0 %collective-permute-start.8 = (f32[11,8,128]{2,1,0:T(8,128)S(1)}, f32[11,8,128]{2,1,0:T(8,128)S(1)}, u32[]{:S(2)}, u32[]{:S(2)}) collective-permute-start(f32[11,8,128]{2,1,0:T(8,128)S(1)} %add_multiply_fusion), channel_id=1, source_target_pairs={{0,4},{4,8},{8,12},{12,0},{1,5},{5,9},{9,13},{13,1},{2,6},{6,10},{... | collective-permute-start | bytes 135176 | tf_op jit(solution)/shard_map/ppermute | solution.py:349
  184.5 40.8 %all-to-all-start.2 = ((bf16[16,2,6,16,256]{4,3,2,1,0:T(8,128)(2,1)}), bf16[16,2,6,16,256]{4,3,2,1,0:T(8,128)(2,1)}, u32[]{:S(2)}, u32[]{:S(2)}) async-start(bf16[16,2,6,16,256]{4,3,2,1,0:T(8,128)(2,1)} %get-tuple-element.23), calls=%async_computation.2 | async-start | bytes 3145728 | tf_op jit(solution)/shard_map/all_to_all | solution.py:436
  190.5 8.0 %collective-permute-start.11 = (f32[11,8,128]{2,1,0:T(8,128)S(1)}, f32[11,8,128]{2,1,0:T(8,128)S(1)}, u32[]{:S(2)}, u32[]{:S(2)}) collective-permute-start(f32[11,8,128]{2,1,0:T(8,128)S(1)} %add_bitcast_fusion), channel_id=1, source_target_pairs={{0,1},{1,2},{2,3},{3,0},{4,5},{5,6},{6,7},{7,4},{8,9},{9,10},{10,1... | collective-permute-start | bytes 135176 | tf_op jit(solution)/shard_map/ppermute | solution.py:349
  192.0 7.3 %collective-permute-start.12 = (f32[11,8,128]{2,1,0:T(8,128)S(1)}, f32[11,8,128]{2,1,0:T(8,128)S(1)}, u32[]{:S(2)}, u32[]{:S(2)}) collective-permute-start(f32[11,8,128]{2,1,0:T(8,128)S(1)} %add_bitcast_fusion), channel_id=1, source_target_pairs={{0,2},{1,3},{2,0},{3,1},{4,6},{5,7},{6,4},{7,5},{8,10},{9,11},{10,... | collective-permute-start | bytes 135176 | tf_op jit(solution)/shard_map/ppermute | solution.py:349
  194.7 4.9 %collective-permute-start.13 = (f32[11,8,128]{2,1,0:T(8,128)S(1)}, f32[11,8,128]{2,1,0:T(8,128)S(1)}, u32[]{:S(2)}, u32[]{:S(2)}) collective-permute-start(f32[11,8,128]{2,1,0:T(8,128)S(1)} %add_bitcast_fusion), channel_id=1, source_target_pairs={{0,3},{1,0},{2,1},{3,2},{4,7},{5,4},{6,5},{7,6},{8,11},{9,8},{10,9... | collective-permute-start | bytes 135176 | tf_op jit(solution)/shard_map/ppermute | solution.py:349
  199.6 9.5 %collective-permute-start.14 = (f32[44,8,128]{2,1,0:T(8,128)S(1)}, f32[44,8,128]{2,1,0:T(8,128)S(1)}, u32[]{:S(2)}, u32[]{:S(2)}) collective-permute-start(f32[44,8,128]{2,1,0:T(8,128)S(1)} %constant_dynamic-update-slice_fusion.3), channel_id=1, source_target_pairs={{0,32},{32,64},{64,96},{96,0},{1,33},{33,65},{65,97},{97,1},{2,34}... | collective-permute-start | bytes 540680 | tf_op jit(solution)/shard_map/ppermute | solution.py:349
  199.6 9.5 %collective-permute-start.15 = (f32[44,8,128]{2,1,0:T(8,128)S(1)}, f32[44,8,128]{2,1,0:T(8,128)S(1)}, u32[]{:S(2)}, u32[]{:S(2)}) collective-permute-start(f32[44,8,128]{2,1,0:T(8,128)S(1)} %constant_dynamic-update-slice_fusion.3), channel_id=1, source_target_pairs={{0,64},{32,96},{64,0},{96,32},{1,65},{33,97},{65,1},{97,33},{2,66}... | collective-permute-start | bytes 540680 | tf_op jit(solution)/shard_map/ppermute | solution.py:349
  202.3 6.9 %collective-permute-start.16 = (f32[44,8,128]{2,1,0:T(8,128)S(1)}, f32[44,8,128]{2,1,0:T(8,128)S(1)}, u32[]{:S(2)}, u32[]{:S(2)}) collective-permute-start(f32[44,8,128]{2,1,0:T(8,128)S(1)} %constant_dynamic-update-slice_fusion.3), channel_id=1, source_target_pairs={{0,96},{32,0},{64,32},{96,64},{1,97},{33,1},{65,33},{97,65},{2,98}... | collective-permute-start | bytes 540680 | tf_op jit(solution)/shard_map/ppermute | solution.py:349
  209.2 2.3 collective-permute-start.17
